TPU v7x, 128 devices: a whole 4x4x4 slice. The times are simulated.
128 devices in a mesh: cuts: 8 (over z, x_lo), space: 16 (over y, x_hi, core).
Axes of the slice: x: 4 (x_hi: 2, x_lo: 2; x = x_hi * 2 + x_lo), y: 4, z: 4, core: 2. Of those that a mesh axis runs over, the one named last changes fastest.
Arguments:
- states: float32 [8, 512, 2048], P('cuts', 'space'), may hold values from -6 to 6
- stream: float32 [512, 2048], P('space'), may hold values from -4 to 4
Outputs:
- new_states: float32 [8, 512, 2048], P('cuts', 'space')
All inputs are finite; a program needn't handle non-finite values.
Results may differ from a plain program's by a relative error of at most 0.00002.
Values sent between devices are 32-bit elements; how exact they have to be, the bound alone decides.
A program may use at most 64 MiB of HBM per device.

v0:
```python
import jax
import jax.numpy as jnp
from jax import lax
from jax.sharding import PartitionSpec as P

FINE_STEPS = 4


VISCOSITY = 0.2
FINE_DT = 0.25


def with_halo(x, sides, width):
    for axis, dim in sides:
        size, length = (lax.axis_size(axis), x.shape[dim])
        up = [(i, (i + 1) % size) for i in range(size)]
        down = [(j, i) for i, j in up]
        last = lax.slice_in_dim(x, length - width, length, axis=dim)
        leading = lax.slice_in_dim(x, 0, width, axis=dim)
        before = lax.ppermute(last, axis, up)
        after = lax.ppermute(leading, axis, down)
        x = jnp.concatenate([before, x, after], axis=dim)
    return x


def passed_along(x, axis, by):
    length = lax.axis_size(axis)
    pairs = [(i, i + by) for i in range(length) if 0 <= i + by < length]
    return lax.ppermute(x, axis, pairs)


def velocity(padded, spacing):
    middle = padded[1:-1]
    speed_x = (padded[2:] - padded[:-2]) / (2.0 * spacing)
    speed_y = -((jnp.roll(middle, -1, 1) - jnp.roll(middle, 1, 1)) / (2.0 * spacing))
    return (speed_x, speed_y)


def tendency(padded, speed_x, speed_y, spacing):
    middle = padded[1:-1]
    right_col = jnp.roll(middle, -1, 1)
    left_col = jnp.roll(middle, 1, 1)
    upper_row = padded[2:]
    lower_row = padded[:-2]
    slope_x = (right_col - left_col) / (2.0 * spacing)
    slope_y = (upper_row - lower_row) / (2.0 * spacing)
    laplace = (upper_row + lower_row + right_col + left_col - 4.0 * middle) / (spacing * spacing)
    return -speed_x * slope_x - speed_y * slope_y + VISCOSITY * laplace


def runge_step(field, speed_x, speed_y, spacing, step_size, pad_fn):
    segment_one = tendency(pad_fn(field), speed_x, speed_y, spacing)
    segment_two = tendency(pad_fn(field + 0.5 * step_size * segment_one), speed_x, speed_y, spacing)
    segment_three = tendency(
        pad_fn(field + 0.5 * step_size * segment_two), speed_x, speed_y, spacing
    )
    segment_four = tendency(pad_fn(field + step_size * segment_three), speed_x, speed_y, spacing)
    return field + step_size / 6.0 * (
        segment_one + 2.0 * segment_two + 2.0 * segment_three + segment_four
    )


def restrict(field):
    leading = field.shape[:-2]
    height, width = field.shape[-2:]
    return field.reshape(leading + (height // 4, 4, width // 4, 4)).mean(axis=(-3, -1))


def prolong(field):
    return jnp.repeat(jnp.repeat(field, 4, axis=-2), 4, axis=-1)


def coarse_pad(field):
    return with_halo(field, (("space", 0),), 1)


def fine_pad(field):
    return with_halo(field, (("space", 0),), 1)


def per_device(states, stream):
    own_state = states[0]
    slice_index = lax.axis_index("cuts")
    slices = lax.axis_size("cuts")
    stream_wide = with_halo(stream, (("space", 0),), 5)
    wide_x, wide_y = velocity(stream_wide, 1.0)
    fine_u = wide_x[4:-4]
    fine_v = wide_y[4:-4]
    coarse_padded = with_halo(restrict(stream), (("space", 0),), 4)
    coarse_wide_x, coarse_wide_y = velocity(coarse_padded, 4.0)
    coarse_u = coarse_wide_x[3:-3]
    coarse_v = coarse_wide_y[3:-3]
    coarse_size = FINE_DT * FINE_STEPS

    def coarse_prop(field):
        return runge_step(field, coarse_u, coarse_v, 4.0, coarse_size, coarse_pad)

    coarse_start = restrict(own_state)
    coarse_old = coarse_prop(coarse_start)
    fine_end = own_state
    for _ in range(FINE_STEPS):
        fine_end = runge_step(fine_end, fine_u, fine_v, 1.0, FINE_DT, fine_pad)
    coarse_gap = restrict(fine_end) - coarse_old

    def handoff(segment, current):
        moved = passed_along(coarse_prop(current) + coarse_gap, "cuts", 1)
        return jnp.where(slice_index == 0, coarse_start, moved)

    current = lax.fori_loop(0, slices - 1, handoff, coarse_start)
    stepped = coarse_prop(current)
    return (fine_end + prolong(stepped - coarse_old))[None]


def solution(mesh):
    in_specs = (P("cuts", "space", None), P("space", None))
    out_specs = P("cuts", "space", None)
    return jax.shard_map(
        per_device, mesh=mesh, in_specs=in_specs, out_specs=out_specs, check_vma=False
    )
```

profile of v0, /device:TPU:64, one launch (start us, length us, event | category | flops | bytes accessed | tf_op | source)
XLA Modules:
  0.0 532.6 jit_solution(7377873793763558619)
XLA Ops:
  5.9 10.9 %reshape.14 = f32[8,4,512,4]{3,2,1,0:T(8,128)} reshape(f32[32,2048]{1,0:T(8,128)} %param.5) | data formatting | bytes 524288 | tf_op jit(solution)/shard_map/reshape | solution.py:66
  26.5 10.0 %reshape_squeeze.3 = f32[8,4,512,4]{3,2,1,0:T(8,128)} reshape(f32[1,32,2048]{2,1,0:T(8,128)S(1)} %copy-done) | data formatting | bytes 524288 | tf_op jit(solution)/shard_map/reshape;squeeze | solution.py:66
  40.7 5.4 %collective-permute-start.45 = (f32[1,512]{1,0:T(1,128)S(1)}, f32[1,512]{1,0:T(1,128)S(1)}, u32[]{:S(2)}, u32[]{:S(2)}) collective-permute-start(f32[1,512]{1,0:T(1,128)S(1)} %get-tuple-element.355), channel_id=1, source_target_pairs={{1,0},{2,1},{3,2},{4,3},{5,4},{6,5},{7,6},{8,7},{9,8},{10,9},{11,1... | collective-permute-start | bytes 6152 | tf_op jit(solution)/shard_map/ppermute | solution.py:21
  62.4 5.5 %collective-permute-start.51 = (f32[1,512]{1,0:T(1,128)S(1)}, f32[1,512]{1,0:T(1,128)S(1)}, u32[]{:S(2)}, u32[]{:S(2)}) collective-permute-start(f32[1,512]{1,0:T(1,128)S(1)} %get-tuple-element.335), channel_id=1, source_target_pairs={{1,0},{2,1},{3,2},{4,3},{5,4},{6,5},{7,6},{8,7},{9,8},{10,9},{11,1... | collective-permute-start | bytes 6152 | tf_op jit(solution)/shard_map/ppermute | solution.py:21
  76.6 5.6 %collective-permute-start.15 = (f32[1,2048]{1,0:T(1,128)S(1)}, f32[1,2048]{1,0:T(1,128)S(1)}, u32[]{:S(2)}, u32[]{:S(2)}) collective-permute-start(f32[1,2048]{1,0:T(1,128)S(1)} %get-tuple-element.285), channel_id=1, source_target_pairs={{1,0},{2,1},{3,2},{4,3},{5,4},{6,5},{7,6},{8,7},{9,8},{10,9},{11,1... | collective-permute-start | bytes 24584 | tf_op jit(solution)/shard_map/ppermute | solution.py:21
  84.0 5.4 %collective-permute-start.17 = (f32[1,2048]{1,0:T(1,128)S(1)}, f32[1,2048]{1,0:T(1,128)S(1)}, u32[]{:S(2)}, u32[]{:S(2)}) collective-permute-start(f32[1,2048]{1,0:T(1,128)S(1)} %get-tuple-element.280), channel_id=1, source_target_pairs={{1,0},{2,1},{3,2},{4,3},{5,4},{6,5},{7,6},{8,7},{9,8},{10,9},{11,1... | collective-permute-start | bytes 24584 | tf_op jit(solution)/shard_map/ppermute | solution.py:21
  98.2 5.4 %collective-permute-done.20 = f32[1,2048]{1,0:T(1,128)S(1)} collective-permute-done((f32[1,2048]{1,0:T(1,128)S(1)}, f32[1,2048]{1,0:T(1,128)S(1)}, u32[]{:S(2)}, u32[]{:S(2)}) %collective-permute-start.20) | collective-permute-done | bytes 8224 | tf_op jit(solution)/shard_map/ppermute | solution.py:20
  111.2 5.4 %collective-permute-start.23 = (f32[1,2048]{1,0:T(1,128)S(1)}, f32[1,2048]{1,0:T(1,128)S(1)}, u32[]{:S(2)}, u32[]{:S(2)}) collective-permute-start(f32[1,2048]{1,0:T(1,128)S(1)} %get-tuple-element.261), channel_id=1, source_target_pairs={{1,0},{2,1},{3,2},{4,3},{5,4},{6,5},{7,6},{8,7},{9,8},{10,9},{11,1... | collective-permute-start | bytes 24584 | tf_op jit(solution)/shard_map/ppermute | solution.py:21
  118.4 5.4 %collective-permute-start.25 = (f32[1,2048]{1,0:T(1,128)S(1)}, f32[1,2048]{1,0:T(1,128)S(1)}, u32[]{:S(2)}, u32[]{:S(2)}) collective-permute-start(f32[1,2048]{1,0:T(1,128)S(1)} %get-tuple-element.256), channel_id=1, source_target_pairs={{1,0},{2,1},{3,2},{4,3},{5,4},{6,5},{7,6},{8,7},{9,8},{10,9},{11,1... | collective-permute-start | bytes 24584 | tf_op jit(solution)/shard_map/ppermute | solution.py:21
  132.5 5.4 %collective-permute-done.28 = f32[1,2048]{1,0:T(1,128)S(1)} collective-permute-done((f32[1,2048]{1,0:T(1,128)S(1)}, f32[1,2048]{1,0:T(1,128)S(1)}, u32[]{:S(2)}, u32[]{:S(2)}) %collective-permute-start.28) | collective-permute-done | bytes 8224 | tf_op jit(solution)/shard_map/ppermute | solution.py:20
  145.6 5.4 %collective-permute-start.31 = (f32[1,2048]{1,0:T(1,128)S(1)}, f32[1,2048]{1,0:T(1,128)S(1)}, u32[]{:S(2)}, u32[]{:S(2)}) collective-permute-start(f32[1,2048]{1,0:T(1,128)S(1)} %get-tuple-element.237), channel_id=1, source_target_pairs={{1,0},{2,1},{3,2},{4,3},{5,4},{6,5},{7,6},{8,7},{9,8},{10,9},{11,1... | collective-permute-start | bytes 24584 | tf_op jit(solution)/shard_map/ppermute | solution.py:21
  152.8 5.4 %collective-permute-start.33 = (f32[1,2048]{1,0:T(1,128)S(1)}, f32[1,2048]{1,0:T(1,128)S(1)}, u32[]{:S(2)}, u32[]{:S(2)}) collective-permute-start(f32[1,2048]{1,0:T(1,128)S(1)} %get-tuple-element.232), channel_id=1, source_target_pairs={{1,0},{2,1},{3,2},{4,3},{5,4},{6,5},{7,6},{8,7},{9,8},{10,9},{11,1... | collective-permute-start | bytes 24584 | tf_op jit(solution)/shard_map/ppermute | solution.py:21
  165.6 9.5 %collective-permute-start.36 = (f32[1,2048]{1,0:T(1,128)S(1)}, f32[1,2048]{1,0:T(1,128)S(1)}, u32[]{:S(2)}, u32[]{:S(2)}) collective-permute-start(f32[1,2048]{1,0:T(1,128)S(1)} %get-tuple-element.225), channel_id=1, source_target_pairs={{0,1},{1,2},{2,3},{3,4},{4,5},{5,6},{6,7},{7,8},{8,9},{9,10},{10,1... | collective-permute-start | bytes 24584 | tf_op jit(solution)/shard_map/ppermute | solution.py:20
  175.2 6.4 %collective-permute-done.36 = f32[1,2048]{1,0:T(1,128)S(1)} collective-permute-done((f32[1,2048]{1,0:T(1,128)S(1)}, f32[1,2048]{1,0:T(1,128)S(1)}, u32[]{:S(2)}, u32[]{:S(2)}) %collective-permute-start.36) | collective-permute-done | bytes 8224 | tf_op jit(solution)/shard_map/ppermute | solution.py:20
  189.3 5.4 %collective-permute-start.39 = (f32[1,2048]{1,0:T(1,128)S(1)}, f32[1,2048]{1,0:T(1,128)S(1)}, u32[]{:S(2)}, u32[]{:S(2)}) collective-permute-start(f32[1,2048]{1,0:T(1,128)S(1)} %get-tuple-element.213), channel_id=1, source_target_pairs={{1,0},{2,1},{3,2},{4,3},{5,4},{6,5},{7,6},{8,7},{9,8},{10,9},{11,1... | collective-permute-start | bytes 24584 | tf_op jit(solution)/shard_map/ppermute | solution.py:21
  196.5 5.4 %collective-permute-start.41 = (f32[1,2048]{1,0:T(1,128)S(1)}, f32[1,2048]{1,0:T(1,128)S(1)}, u32[]{:S(2)}, u32[]{:S(2)}) collective-permute-start(f32[1,2048]{1,0:T(1,128)S(1)} %get-tuple-element.208), channel_id=1, source_target_pairs={{1,0},{2,1},{3,2},{4,3},{5,4},{6,5},{7,6},{8,7},{9,8},{10,9},{11,1... | collective-permute-start | bytes 24584 | tf_op jit(solution)/shard_map/ppermute | solution.py:21
  209.0 10.0 %reshape.15 = f32[8,4,512,4]{3,2,1,0:T(8,128)} reshape(f32[32,2048]{1,0:T(8,128)S(1)} %multiply_add_fusion.5) | data formatting | bytes 524288 | tf_op jit(solution)/shard_map/reshape | solution.py:66
  223.2 275.0 %while.13 = (s32[]{:T(128)}, f32[8,512]{1,0:T(8,128)S(1)}, pred[]{:T(512)}, f32[8,512]{1,0:T(8,128)S(1)}, f32[8,512]{1,0:T(8,128)S(1)}, /*index=5*/f32[8,512]{1,0:T(8,128)S(1)}, f32[8,512]{1,0:T(8,128)S(1)}, s32[]{:T(128)}) while((s32[]{:T(128)}, f32[8,512]{1,0:T(8,128)S(1)}, pred[]{:T(512)}, f32[8,512]{1,0:T(8,128)S(1)}, ...), condition=%wide.region_4.5_spmd, body=%wide.region_3.4_spmd.sunk | while | flops 425986 | bytes 1053118 | solution.py:109
  224.6 5.4 %collective-permute-done.1 = f32[1,512]{1,0:T(1,128)S(1)} collective-permute-done((f32[1,512]{1,0:T(1,128)S(1)}, f32[1,512]{1,0:T(1,128)S(1)}, u32[]{:S(2)}, u32[]{:S(2)}) %collective-permute-start.1) | collective-permute-done | bytes 2080 | tf_op jit(solution)/shard_map/while/body/eval_jaxpr/ppermute | solution.py:20
  263.9 5.4 %collective-permute-done.1 = f32[1,512]{1,0:T(1,128)S(1)} collective-permute-done((f32[1,512]{1,0:T(1,128)S(1)}, f32[1,512]{1,0:T(1,128)S(1)}, u32[]{:S(2)}, u32[]{:S(2)}) %collective-permute-start.1) | collective-permute-done | bytes 2080 | tf_op jit(solution)/shard_map/while/body/eval_jaxpr/ppermute | solution.py:20
  303.2 5.4 %collective-permute-done.1 = f32[1,512]{1,0:T(1,128)S(1)} collective-permute-done((f32[1,512]{1,0:T(1,128)S(1)}, f32[1,512]{1,0:T(1,128)S(1)}, u32[]{:S(2)}, u32[]{:S(2)}) %collective-permute-start.1) | collective-permute-done | bytes 2080 | tf_op jit(solution)/shard_map/while/body/eval_jaxpr/ppermute | solution.py:20
  342.5 5.4 %collective-permute-done.1 = f32[1,512]{1,0:T(1,128)S(1)} collective-permute-done((f32[1,512]{1,0:T(1,128)S(1)}, f32[1,512]{1,0:T(1,128)S(1)}, u32[]{:S(2)}, u32[]{:S(2)}) %collective-permute-start.1) | collective-permute-done | bytes 2080 | tf_op jit(solution)/shard_map/while/body/eval_jaxpr/ppermute | solution.py:20
  421.1 5.4 %collective-permute-done.1 = f32[1,512]{1,0:T(1,128)S(1)} collective-permute-done((f32[1,512]{1,0:T(1,128)S(1)}, f32[1,512]{1,0:T(1,128)S(1)}, u32[]{:S(2)}, u32[]{:S(2)}) %collective-permute-start.1) | collective-permute-done | bytes 2080 | tf_op jit(solution)/shard_map/while/body/eval_jaxpr/ppermute | solution.py:20
  460.4 5.4 %collective-permute-done.1 = f32[1,512]{1,0:T(1,128)S(1)} collective-permute-done((f32[1,512]{1,0:T(1,128)S(1)}, f32[1,512]{1,0:T(1,128)S(1)}, u32[]{:S(2)}, u32[]{:S(2)}) %collective-permute-start.1) | collective-permute-done | bytes 2080 | tf_op jit(solution)/shard_map/while/body/eval_jaxpr/ppermute | solution.py:20
  (450 shorter events, 386.7 us)
Async XLA Ops:
  0.9 67.8 %collective-permute-start.11 = (f32[1,2048]{1,0:T(1,128)S(1)}, f32[1,2048]{1,0:T(1,128)S(1)}, u32[]{:S(2)}, u32[]{:S(2)}) collective-permute-start(f32[1,2048]{1,0:T(1,128)S(1)} %get-tuple-element.300), channel_id=1, source_target_pairs={{1,0},{2,1},{3,2},{4,3},{5,4},{6,5},{7,6},{8,7},{9,8},{10,9},{11,1... | collective-permute-start | bytes 24584 | tf_op jit(solution)/shard_map/ppermute | solution.py:21
  5.9 62.9 %collective-permute-start.12 = (f32[1,2048]{1,0:T(1,128)S(1)}, f32[1,2048]{1,0:T(1,128)S(1)}, u32[]{:S(2)}, u32[]{:S(2)}) collective-permute-start(f32[1,2048]{1,0:T(1,128)S(1)} %get-tuple-element.299), channel_id=1, source_target_pairs={{0,1},{1,2},{2,3},{3,4},{4,5},{5,6},{6,7},{7,8},{8,9},{9,10},{10,1... | collective-permute-start | bytes 24584 | tf_op jit(solution)/shard_map/ppermute | solution.py:20
  20.9 19.9 %collective-permute-start.44 = (f32[4,512]{1,0:T(4,128)S(1)}, f32[4,512]{1,0:T(4,128)S(1)}, u32[]{:S(2)}, u32[]{:S(2)}) collective-permute-start(f32[4,512]{1,0:T(4,128)S(1)} %get-tuple-element.350), channel_id=1, source_target_pairs={{1,0},{2,1},{3,2},{4,3},{5,4},{6,5},{7,6},{8,7},{9,8},{10,9},{11,1... | collective-permute-start | bytes 24584 | tf_op jit(solution)/shard_map/ppermute | solution.py:21
  26.2 19.9 %collective-permute-start.43 = (f32[4,512]{1,0:T(4,128)S(1)}, f32[4,512]{1,0:T(4,128)S(1)}, u32[]{:S(2)}, u32[]{:S(2)}) collective-permute-start(f32[4,512]{1,0:T(4,128)S(1)} %get-tuple-element.349), channel_id=1, source_target_pairs={{0,1},{1,2},{2,3},{3,4},{4,5},{5,6},{6,7},{7,8},{8,9},{9,10},{10,1... | collective-permute-start | bytes 24584 | tf_op jit(solution)/shard_map/ppermute | solution.py:20
  61.2 7.3 %collective-permute-start.9 = (f32[5,2048]{1,0:T(8,128)S(1)}, f32[5,2048]{1,0:T(8,128)S(1)}, u32[]{:S(2)}, u32[]{:S(2)}) collective-permute-start(f32[5,2048]{1,0:T(8,128)S(1)} %get-tuple-element.293), channel_id=1, source_target_pairs={{0,1},{1,2},{2,3},{3,4},{4,5},{5,6},{6,7},{7,8},{8,9},{9,10},{10,1... | collective-permute-start | bytes 122888 | tf_op jit(solution)/shard_map/ppermute | solution.py:20
  61.5 161.6 %collective-permute-start.52 = (f32[1,512]{1,0:T(1,128)S(1)}, f32[1,512]{1,0:T(1,128)S(1)}, u32[]{:S(2)}, u32[]{:S(2)}) collective-permute-start(f32[1,512]{1,0:T(1,128)S(1)} %get-tuple-element.336), channel_id=1, source_target_pairs={{0,1},{1,2},{2,3},{3,4},{4,5},{5,6},{6,7},{7,8},{8,9},{9,10},{10,1... | collective-permute-start | bytes 6152 | tf_op jit(solution)/shard_map/ppermute | solution.py:20
  62.4 160.7 %collective-permute-start.51 = (f32[1,512]{1,0:T(1,128)S(1)}, f32[1,512]{1,0:T(1,128)S(1)}, u32[]{:S(2)}, u32[]{:S(2)}) collective-permute-start(f32[1,512]{1,0:T(1,128)S(1)} %get-tuple-element.335), channel_id=1, source_target_pairs={{1,0},{2,1},{3,2},{4,3},{5,4},{6,5},{7,6},{8,7},{9,8},{10,9},{11,1... | collective-permute-start | bytes 6152 | tf_op jit(solution)/shard_map/ppermute | solution.py:21
  69.3 6.8 %collective-permute-start.14 = (f32[1,2048]{1,0:T(1,128)S(1)}, f32[1,2048]{1,0:T(1,128)S(1)}, u32[]{:S(2)}, u32[]{:S(2)}) collective-permute-start(f32[1,2048]{1,0:T(1,128)S(1)} %get-tuple-element.292), channel_id=1, source_target_pairs={{0,1},{1,2},{2,3},{3,4},{4,5},{5,6},{6,7},{7,8},{8,9},{9,10},{10,1... | collective-permute-start | bytes 24584 | tf_op jit(solution)/shard_map/ppermute | solution.py:20
  76.5 6.8 %collective-permute-start.16 = (f32[1,2048]{1,0:T(1,128)S(1)}, f32[1,2048]{1,0:T(1,128)S(1)}, u32[]{:S(2)}, u32[]{:S(2)}) collective-permute-start(f32[1,2048]{1,0:T(1,128)S(1)} %get-tuple-element.286), channel_id=1, source_target_pairs={{0,1},{1,2},{2,3},{3,4},{4,5},{5,6},{6,7},{7,8},{8,9},{9,10},{10,1... | collective-permute-start | bytes 24584 | tf_op jit(solution)/shard_map/ppermute | solution.py:20
  76.6 7.0 %collective-permute-start.15 = (f32[1,2048]{1,0:T(1,128)S(1)}, f32[1,2048]{1,0:T(1,128)S(1)}, u32[]{:S(2)}, u32[]{:S(2)}) collective-permute-start(f32[1,2048]{1,0:T(1,128)S(1)} %get-tuple-element.285), channel_id=1, source_target_pairs={{1,0},{2,1},{3,2},{4,3},{5,4},{6,5},{7,6},{8,7},{9,8},{10,9},{11,1... | collective-permute-start | bytes 24584 | tf_op jit(solution)/shard_map/ppermute | solution.py:21
  84.0 6.8 %collective-permute-start.17 = (f32[1,2048]{1,0:T(1,128)S(1)}, f32[1,2048]{1,0:T(1,128)S(1)}, u32[]{:S(2)}, u32[]{:S(2)}) collective-permute-start(f32[1,2048]{1,0:T(1,128)S(1)} %get-tuple-element.280), channel_id=1, source_target_pairs={{1,0},{2,1},{3,2},{4,3},{5,4},{6,5},{7,6},{8,7},{9,8},{10,9},{11,1... | collective-permute-start | bytes 24584 | tf_op jit(solution)/shard_map/ppermute | solution.py:21
  96.8 6.8 %collective-permute-start.20 = (f32[1,2048]{1,0:T(1,128)S(1)}, f32[1,2048]{1,0:T(1,128)S(1)}, u32[]{:S(2)}, u32[]{:S(2)}) collective-permute-start(f32[1,2048]{1,0:T(1,128)S(1)} %get-tuple-element.273), channel_id=1, source_target_pairs={{0,1},{1,2},{2,3},{3,4},{4,5},{5,6},{6,7},{7,8},{8,9},{9,10},{10,1... | collective-permute-start | bytes 24584 | tf_op jit(solution)/shard_map/ppermute | solution.py:20
  104.0 6.8 %collective-permute-start.22 = (f32[1,2048]{1,0:T(1,128)S(1)}, f32[1,2048]{1,0:T(1,128)S(1)}, u32[]{:S(2)}, u32[]{:S(2)}) collective-permute-start(f32[1,2048]{1,0:T(1,128)S(1)} %get-tuple-element.268), channel_id=1, source_target_pairs={{0,1},{1,2},{2,3},{3,4},{4,5},{5,6},{6,7},{7,8},{8,9},{9,10},{10,1... | collective-permute-start | bytes 24584 | tf_op jit(solution)/shard_map/ppermute | solution.py:20
  111.2 6.8 %collective-permute-start.24 = (f32[1,2048]{1,0:T(1,128)S(1)}, f32[1,2048]{1,0:T(1,128)S(1)}, u32[]{:S(2)}, u32[]{:S(2)}) collective-permute-start(f32[1,2048]{1,0:T(1,128)S(1)} %get-tuple-element.262), channel_id=1, source_target_pairs={{0,1},{1,2},{2,3},{3,4},{4,5},{5,6},{6,7},{7,8},{8,9},{9,10},{10,1... | collective-permute-start | bytes 24584 | tf_op jit(solution)/shard_map/ppermute | solution.py:20
  118.4 6.8 %collective-permute-start.25 = (f32[1,2048]{1,0:T(1,128)S(1)}, f32[1,2048]{1,0:T(1,128)S(1)}, u32[]{:S(2)}, u32[]{:S(2)}) collective-permute-start(f32[1,2048]{1,0:T(1,128)S(1)} %get-tuple-element.256), channel_id=1, source_target_pairs={{1,0},{2,1},{3,2},{4,3},{5,4},{6,5},{7,6},{8,7},{9,8},{10,9},{11,1... | collective-permute-start | bytes 24584 | tf_op jit(solution)/shard_map/ppermute | solution.py:21
  131.2 6.8 %collective-permute-start.28 = (f32[1,2048]{1,0:T(1,128)S(1)}, f32[1,2048]{1,0:T(1,128)S(1)}, u32[]{:S(2)}, u32[]{:S(2)}) collective-permute-start(f32[1,2048]{1,0:T(1,128)S(1)} %get-tuple-element.249), channel_id=1, source_target_pairs={{0,1},{1,2},{2,3},{3,4},{4,5},{5,6},{6,7},{7,8},{8,9},{9,10},{10,1... | collective-permute-start | bytes 24584 | tf_op jit(solution)/shard_map/ppermute | solution.py:20
  138.3 6.8 %collective-permute-start.30 = (f32[1,2048]{1,0:T(1,128)S(1)}, f32[1,2048]{1,0:T(1,128)S(1)}, u32[]{:S(2)}, u32[]{:S(2)}) collective-permute-start(f32[1,2048]{1,0:T(1,128)S(1)} %get-tuple-element.244), channel_id=1, source_target_pairs={{0,1},{1,2},{2,3},{3,4},{4,5},{5,6},{6,7},{7,8},{8,9},{9,10},{10,1... | collective-permute-start | bytes 24584 | tf_op jit(solution)/shard_map/ppermute | solution.py:20
  145.5 6.8 %collective-permute-start.32 = (f32[1,2048]{1,0:T(1,128)S(1)}, f32[1,2048]{1,0:T(1,128)S(1)}, u32[]{:S(2)}, u32[]{:S(2)}) collective-permute-start(f32[1,2048]{1,0:T(1,128)S(1)} %get-tuple-element.238), channel_id=1, source_target_pairs={{0,1},{1,2},{2,3},{3,4},{4,5},{5,6},{6,7},{7,8},{8,9},{9,10},{10,1... | collective-permute-start | bytes 24584 | tf_op jit(solution)/shard_map/ppermute | solution.py:20
  152.8 6.8 %collective-permute-start.33 = (f32[1,2048]{1,0:T(1,128)S(1)}, f32[1,2048]{1,0:T(1,128)S(1)}, u32[]{:S(2)}, u32[]{:S(2)}) collective-permute-start(f32[1,2048]{1,0:T(1,128)S(1)} %get-tuple-element.232), channel_id=1, source_target_pairs={{1,0},{2,1},{3,2},{4,3},{5,4},{6,5},{7,6},{8,7},{9,8},{10,9},{11,1... | collective-permute-start | bytes 24584 | tf_op jit(solution)/shard_map/ppermute | solution.py:21
  165.5 9.7 %collective-permute-start.35 = (f32[1,2048]{1,0:T(1,128)S(1)}, f32[1,2048]{1,0:T(1,128)S(1)}, u32[]{:S(2)}, u32[]{:S(2)}) collective-permute-start(f32[1,2048]{1,0:T(1,128)S(1)} %get-tuple-element.226), channel_id=1, source_target_pairs={{1,0},{2,1},{3,2},{4,3},{5,4},{6,5},{7,6},{8,7},{9,8},{10,9},{11,1... | collective-permute-start | bytes 24584 | tf_op jit(solution)/shard_map/ppermute | solution.py:21
  165.6 16.1 %collective-permute-start.36 = (f32[1,2048]{1,0:T(1,128)S(1)}, f32[1,2048]{1,0:T(1,128)S(1)}, u32[]{:S(2)}, u32[]{:S(2)}) collective-permute-start(f32[1,2048]{1,0:T(1,128)S(1)} %get-tuple-element.225), channel_id=1, source_target_pairs={{0,1},{1,2},{2,3},{3,4},{4,5},{5,6},{6,7},{7,8},{8,9},{9,10},{10,1... | collective-permute-start | bytes 24584 | tf_op jit(solution)/shard_map/ppermute | solution.py:20
  182.0 6.8 %collective-permute-start.38 = (f32[1,2048]{1,0:T(1,128)S(1)}, f32[1,2048]{1,0:T(1,128)S(1)}, u32[]{:S(2)}, u32[]{:S(2)}) collective-permute-start(f32[1,2048]{1,0:T(1,128)S(1)} %get-tuple-element.220), channel_id=1, source_target_pairs={{0,1},{1,2},{2,3},{3,4},{4,5},{5,6},{6,7},{7,8},{8,9},{9,10},{10,1... | collective-permute-start | bytes 24584 | tf_op jit(solution)/shard_map/ppermute | solution.py:20
  189.2 6.8 %collective-permute-start.40 = (f32[1,2048]{1,0:T(1,128)S(1)}, f32[1,2048]{1,0:T(1,128)S(1)}, u32[]{:S(2)}, u32[]{:S(2)}) collective-permute-start(f32[1,2048]{1,0:T(1,128)S(1)} %get-tuple-element.214), channel_id=1, source_target_pairs={{0,1},{1,2},{2,3},{3,4},{4,5},{5,6},{6,7},{7,8},{8,9},{9,10},{10,1... | collective-permute-start | bytes 24584 | tf_op jit(solution)/shard_map/ppermute | solution.py:20
  196.5 6.8 %collective-permute-start.41 = (f32[1,2048]{1,0:T(1,128)S(1)}, f32[1,2048]{1,0:T(1,128)S(1)}, u32[]{:S(2)}, u32[]{:S(2)}) collective-permute-start(f32[1,2048]{1,0:T(1,128)S(1)} %get-tuple-element.208), channel_id=1, source_target_pairs={{1,0},{2,1},{3,2},{4,3},{5,4},{6,5},{7,6},{8,7},{9,8},{10,9},{11,1... | collective-permute-start | bytes 24584 | tf_op jit(solution)/shard_map/ppermute | solution.py:21
  (93 other events, 589.4 us)
where the time goes:
time: 537 us; the launch traced here: 533 us
  starting transfers between devices  256 us (48%)
  waiting for transfers between devices  213 us (40%)
  local copies, waits for them, and re-layouts  41.8 us (8%)
  other arithmetic  20.9 us (4%)
    ppermute x54, starting transfers between devices, with_halo(): after = lax.ppermute(leading, axis, down)  226 us
    ppermute x54, waiting for transfers between devices, with_halo(): before = lax.ppermute(last, axis, up)  156 us
    ppermute x7, waiting for transfers between devices, passed_along(): return lax.ppermute(x, axis, pairs)  31.6 us
    ppermute x54, waiting for transfers between devices, with_halo(): after = lax.ppermute(leading, axis, down)  24.9 us
    reshape x2, local copies, waits for them, and re-layouts, restrict(): field.reshape(leading + (height // 4, 4, width // 4, 4)).mean(axis=(-3, -1))  21 us
    ppermute x54, starting transfers between devices, with_halo(): before = lax.ppermute(last, axis, up)  15.5 us
    ppermute x7, starting transfers between devices, passed_along(): return lax.ppermute(x, axis, pairs)  14 us
    reduce_sum x3, other arithmetic, restrict(): field.reshape(leading + (height // 4, 4, width // 4, 4)).mean(axis=(-3, -1))  12.1 us
  transfers between devices with their start and end apart: 115, of which 96 were waited for; matrix products, arithmetic and copies ran while one was open for 10% of the time, Pallas kernels for 0%

commit v1 on v0

v1 whole, which is shorter than its diff:
```python
import jax
import jax.numpy as jnp
from jax import lax
from jax.experimental import pallas as pl
from jax.experimental.pallas import tpu as pltpu
from jax.sharding import PartitionSpec as P

MESH = pl.DeviceIdType.MESH
LANES = 128
COLS = 2048
FT = COLS // LANES
CT = FT // 4
BAND = 32
HALO = 16
WIDE = BAND + 2 * HALO
SLICES = 8
SPACE = 16
REACH = 4
CROWS = 8
CWIDE = CROWS * (2 * REACH + 1)
FINE_STEPS = 4
F32 = jnp.float32


def scales(step, kappa):
    gains = [step / (4 - s) / kappa for s in range(4)]
    betas = [1.0] * 4
    for s in (2, 1, 0):
        betas[s] = betas[s + 1] * gains[s + 1]
    return betas, betas[0] * gains[0]


FINE_BETAS, FINE_START = scales(0.25, 1.25)
COARSE_BETAS, COARSE_START = scales(1.0, 20.0)


def rows_up(t):
    return jnp.concatenate([t[1:], pltpu.roll(t[:1], 7, 1)], axis=0)


def rows_down(t):
    return jnp.concatenate([pltpu.roll(t[-1:], 1, 1), t[:-1]], axis=0)


def columns(left, t, right):
    lane = lax.broadcasted_iota(jnp.int32, t.shape, 2)
    west = jnp.where(lane == 0, pltpu.roll(left, 1, 2), pltpu.roll(t, 1, 2))
    east = jnp.where(lane == LANES - 1, pltpu.roll(right, LANES - 1, 2), pltpu.roll(t, LANES - 1, 2))
    return east, west


def coefficients(psi, east, west):
    ce = 0.25 - 0.3125 * (rows_up(psi) - rows_down(psi))
    cn = 0.25 + 0.3125 * (east - west)
    return ce, cn


def operator(t, east, west, ce, cw, cn, cs):
    return ce * east + cw * west + cn * rows_up(t) + cs * rows_down(t) - t


def matmul(x, m):
    return jnp.dot(x, m, precision=lax.Precision.HIGHEST, preferred_element_type=F32)


def kernel(
    states, stream, out,
    xwin, swin, base, ta, tb, fce, fcw, fcn, fcs, shrink, grow, rows, cbuf, wstream, wgap, spw, pay, nbuf, newc,
    local_sem, halo_send, halo_recv, sc_send, sc_recv, a_send, a_recv, b_send, b_recv, c_send, c_recv,
):
    n = lax.axis_index("cuts")
    b = lax.axis_index("space")

    def at_space(j):
        return (n, lax.rem(b + (SPACE + j), SPACE))

    offsets = [j for d in range(1, REACH + 1) for j in (-d, d)]

    own_x = pltpu.make_async_copy(states, xwin.at[pl.ds(HALO // 8, BAND // 8)], local_sem.at[0])
    own_s = pltpu.make_async_copy(stream, swin.at[pl.ds(HALO // 8, BAND // 8)], local_sem.at[1])
    xrows = xwin.reshape(WIDE * FT, LANES)
    srows = swin.reshape(WIDE * FT, LANES)
    own_s.start()
    own_x.start()

    pay[...] = jnp.zeros_like(pay)
    newc[...] = jnp.zeros_like(newc)

    barrier = pltpu.get_barrier_semaphore()
    for j in offsets:
        pl.semaphore_signal(barrier, inc=1, device_id=at_space(j), device_id_type=MESH)
    for k in range(1, SLICES):
        pl.semaphore_signal(
            barrier, inc=1, device_id=(lax.rem(n + k, SLICES), b), device_id_type=MESH
        )
    pl.semaphore_wait(barrier, len(offsets) + SLICES - 1)

    halos = []
    for at, (source, window) in enumerate(((stream, swin), (states, xwin))):
        for side, (j, first, target) in enumerate(((1, BAND - HALO, 0), (-1, 0, HALO + BAND))):
            halos.append(
                pltpu.make_async_remote_copy(
                    src_ref=source.at[pl.ds(first // 8, HALO // 8)],
                    dst_ref=window.at[pl.ds(target // 8, HALO // 8)],
                    send_sem=halo_send.at[2 * at + side],
                    recv_sem=halo_recv.at[2 * at + side],
                    device_id=at_space(j),
                    device_id_type=MESH,
                )
            )
            halos[-1].start()

    fine_at = lax.broadcasted_iota(jnp.int32, (4 * LANES, LANES), 0)
    coarse_at = lax.broadcasted_iota(jnp.int32, (4 * LANES, LANES), 1)
    shrink[...] = jnp.where((fine_at >> 2) == coarse_at, 0.0625, 0.0).astype(F32)
    fine_at = lax.broadcasted_iota(jnp.int32, (LANES, 4 * LANES), 1)
    coarse_at = lax.broadcasted_iota(jnp.int32, (LANES, 4 * LANES), 0)
    grow[...] = jnp.where((fine_at >> 2) == coarse_at, 1.0, 0.0).astype(F32)

    def windows(tiles, target):
        lane = lax.broadcasted_iota(jnp.int32, (CROWS, LANES), 1)
        right = [pltpu.roll(t, 32, 1) for t in tiles]
        left = [pltpu.roll(t, LANES - 32, 1) for t in tiles]
        for j in range(CT):
            target[2 * j] = jnp.where(lane < 32, right[(j - 1) % CT], right[j])
            target[2 * j + 1] = jnp.where(lane < LANES - 32, left[j], left[(j + 1) % CT])

    own_s.wait()
    for c in range(CT):
        for m in range(4):
            for half in range(2):
                parts = [srows[pl.ds(2 * FT * 8 + (4 * c + m) * 8 + 4 * half + i, 4, stride=FT * 8)] for i in range(4)]
                rows[pl.ds(8 * c + 4 * half, 4), pl.ds(m * LANES, LANES)] = parts[0] + parts[1] + parts[2] + parts[3]
    small = matmul(rows[pl.ds(0, CROWS * CT)], shrink[...])
    for c in range(CT):
        for half in range(2):
            cbuf[c, pl.ds(half, 4, stride=2)] = small[8 * c + 4 * half:8 * c + 4 * half + 4]
    windows([cbuf[c, pl.ds(0, CROWS)] for c in range(CT)], wstream)
    spreads = []
    for at, j in enumerate(offsets):
        spreads.append(
            pltpu.make_async_remote_copy(
                src_ref=wstream.at[n],
                dst_ref=spw.at[pl.ds(CROWS * (REACH - j), CROWS)],
                send_sem=sc_send.at[at],
                recv_sem=sc_recv.at[at],
                device_id=at_space(j),
                device_id_type=MESH,
            )
        )
        spreads[-1].start()
    spw[pl.ds(CROWS * REACH, CROWS)] = wstream[n]
    own_x.wait()

    for halo in halos[:2]:
        halo.wait_recv()

    def window_tile(window, c):
        return jnp.stack(
            [window[pl.ds(c * 8 + r, 8, stride=FT * 8)] for r in range(8)]
        )

    def weights(c, carry):
        psi = window_tile(srows, c)
        east, west = columns(
            window_tile(srows, lax.rem(c + FT - 1, FT)), psi, window_tile(srows, lax.rem(c + 1, FT))
        )
        ce, cn = coefficients(psi, east, west)
        fce[c] = ce
        fcw[c] = 0.5 - ce
        fcn[c] = cn
        fcs[c] = 0.5 - cn
        return carry

    lax.fori_loop(0, FT, weights, 0)

    for halo in halos[2:]:
        halo.wait_recv()

    def begin(c, carry):
        base[c] = window_tile(xrows, c)
        return carry

    lax.fori_loop(0, FT, begin, 0)

    def restrict(tile):
        for c in range(CT):
            for m in range(4):
                t = tile(4 * c + m)
                for q in range(2):
                    rows[pl.ds(8 * (2 * c + q), 8), pl.ds(m * LANES, LANES)] = (
                        t[4 * q] + t[4 * q + 1] + t[4 * q + 2] + t[4 * q + 3]
                    )
        small = matmul(rows[...], shrink[...])
        return [
            jnp.stack([small[8 * (2 * c + q):8 * (2 * c + q + 1)] for q in range(2)]) for c in range(CT)
        ]

    cpsi = restrict(lambda c: window_tile(srows, c))
    cweights = []
    for c in range(CT):
        east, west = columns(cpsi[c - 1], cpsi[c], cpsi[(c + 1) % CT])
        ce, cn = coefficients(cpsi[c], east, west)
        cweights.append((ce, 0.5 - ce, cn, 0.5 - cn))
    start = restrict(lambda c: base[c])
    old = start
    for s in range(4):
        moved = []
        for c in range(CT):
            east, west = columns(old[c - 1], old[c], old[(c + 1) % CT])
            change = operator(old[c], east, west, *cweights[c])
            if s == 0:
                change = COARSE_START * change
            moved.append(COARSE_BETAS[s] * start[c] + change)
        old = moved

    def fine_stage(s, src, dst):
        def tile(c, carry):
            t = src[c]
            east, west = columns(src[lax.rem(c + FT - 1, FT)], t, src[lax.rem(c + 1, FT)])
            change = operator(t, east, west, fce[c], fcw[c], fcn[c], fcs[c])
            if s == 0:
                change = FINE_START * change
            dst[c] = FINE_BETAS[s] * base[c] + change
            return carry

        lax.fori_loop(0, FT, tile, 0)

    def fine_step(step, carry):
        fine_stage(0, base, ta)
        fine_stage(1, ta, tb)
        fine_stage(2, tb, ta)
        fine_stage(3, ta, base)
        return carry

    lax.fori_loop(0, FINE_STEPS, fine_step, 0)

    ended = restrict(lambda c: base[c])
    gap = [ended[c] - old[c] for c in range(CT)]
    gap = [jnp.where(n == 0, old[c] + gap[c], gap[c]) for c in range(CT)]
    for c in range(CT):
        for q in range(2):
            cbuf[c, pl.ds(4 + q, 8, stride=2)] = gap[c][q]
    windows([cbuf[c, pl.ds(8, CROWS)] for c in range(CT)], wgap)

    middle = pl.ds(CROWS * REACH, CROWS)

    def gap_copy(k, m):
        return pltpu.make_async_remote_copy(
            src_ref=wgap.at[k],
            dst_ref=pay.at[m, middle],
            send_sem=a_send.at[k],
            recv_sem=a_recv.at[m],
            device_id=(k, b),
            device_id_type=MESH,
        )

    for k in range(SLICES):
        @pl.when((n != k) & (n < SLICES - 1))
        def _():
            gap_copy(k, n).start()

    @pl.when(n < SLICES - 1)
    def _():
        pay[n, middle] = wgap[n]

    for spread in spreads:
        spread.wait()
    psi = jnp.stack([spw[pl.ds(4 + r, 8, stride=8)] for r in range(8)])
    ce, cn = coefficients(psi, pltpu.roll(psi, LANES - 1, 2), pltpu.roll(psi, 1, 2))
    chain_weights = (ce, 0.5 - ce, cn, 0.5 - cn)

    for m in range(SLICES - 1):
        @pl.when(n != m)
        def _():
            gap_copy(m, m).wait_recv()

    gathers = []
    for at, j in enumerate(offsets):
        count = SLICES + 1 - 2 * abs(j)
        gathers.append(
            pltpu.make_async_remote_copy(
                src_ref=pay.at[pl.ds(0, count), middle],
                dst_ref=pay.at[pl.ds(0, count), pl.ds(CROWS * (REACH - j), CROWS)],
                send_sem=b_send.at[at],
                recv_sem=b_recv.at[at],
                device_id=at_space(j),
                device_id_type=MESH,
            )
        )
        gathers[-1].start()
    for gather in gathers:
        gather.wait_recv()

    def new_copy(i, k):
        return pltpu.make_async_remote_copy(
            src_ref=nbuf.at[i, middle],
            dst_ref=newc.at[k],
            send_sem=c_send.at[i],
            recv_sem=c_recv.at[k],
            device_id=(i, b),
            device_id_type=MESH,
        )

    def link(i, current):
        t = current
        for s in range(4):
            change = operator(t, pltpu.roll(t, LANES - 1, 2), pltpu.roll(t, 1, 2), *chain_weights)
            if s == 0:
                change = COARSE_START * change
            t = COARSE_BETAS[s] * current + change
        for r in range(8):
            nbuf[i, pl.ds(4 + r, 8, stride=8)] = t[r]

        @pl.when(i != n)
        def _():
            new_copy(i, n).start()

        @pl.when(i == n)
        def _():
            newc[n] = nbuf[i, middle]

        late = lax.rem(i, SLICES - 1)
        return t + jnp.stack([pay[late, pl.ds(4 + r, 8, stride=8)] for r in range(8)])

    first = jnp.stack([pay[0, pl.ds(4 + r, 8, stride=8)] for r in range(8)])
    lax.fori_loop(1, SLICES, link, first)

    for k in range(SLICES):
        @pl.when((n != k) & (n > 0))
        def _():
            new_copy(k, k).wait_recv()

    lane = lax.broadcasted_iota(jnp.int32, (CROWS, LANES), 1)
    for c in range(CT):
        cbuf[c, pl.ds(8, CROWS)] = jnp.where(
            lane < LANES // 2, pltpu.roll(newc[2 * c], LANES - 32, 1), pltpu.roll(newc[2 * c + 1], 32, 1)
        )
    parts = []
    for c in range(CT):
        for q in range(2):
            new = cbuf[c, pl.ds(4 + q, 8, stride=2)]
            new = jnp.where(n == 0, old[c][q], new)
            parts.append(new - old[c][q])
    rows[...] = matmul(jnp.concatenate(parts, axis=0), grow[...])
    for c in range(CT):
        for m in range(4):
            t = base[4 * c + m]
            for r in range(8):
                xrows[pl.ds((4 * c + m) * 8 + r, 8, stride=FT * 8)] = (
                    t[r] + rows[pl.ds(8 * (2 * c + r // 4), 8), pl.ds(m * LANES, LANES)]
                )
    result = pltpu.make_async_copy(xwin.at[pl.ds(HALO // 8, BAND // 8)], out, local_sem.at[0])
    result.start()

    for halo in halos:
        halo.wait_send()
    for k in range(SLICES):
        @pl.when((n != k) & (n < SLICES - 1))
        def _():
            gap_copy(k, n).wait_send()
    for gather in gathers:
        gather.wait_send()
    for i in range(1, SLICES):
        @pl.when(n != i)
        def _():
            new_copy(i, n).wait_send()
    result.wait()


def per_device(states, stream):
    tiles = pltpu.VMEM((FT, 8, 8, LANES), F32)

    def tiled(x):
        return x.reshape(BAND // 8, 8, FT, LANES).transpose(0, 2, 1, 3)

    ended = pl.pallas_call(
        kernel,
        out_shape=jax.ShapeDtypeStruct((BAND // 8, FT, 8, LANES), F32),
        in_specs=[pl.BlockSpec(memory_space=pl.ANY)] * 2,
        out_specs=pl.BlockSpec(memory_space=pl.ANY),
        scratch_shapes=[
            pltpu.VMEM((WIDE // 8, FT, 8, LANES), F32),
            pltpu.VMEM((WIDE // 8, FT, 8, LANES), F32),
            tiles, tiles, tiles, tiles, tiles, tiles, tiles,
            pltpu.VMEM((4 * LANES, LANES), F32),
            pltpu.VMEM((LANES, 4 * LANES), F32),
            pltpu.VMEM((2 * CT * 8, 4 * LANES), F32),
            pltpu.VMEM((CT, 24, LANES), F32),
            pltpu.VMEM((SLICES, CROWS, LANES), F32),
            pltpu.VMEM((SLICES, CROWS, LANES), F32),
            pltpu.VMEM((CWIDE, LANES), F32),
            pltpu.VMEM((SLICES - 1, CWIDE, LANES), F32),
            pltpu.VMEM((SLICES, CWIDE, LANES), F32),
            pltpu.VMEM((SLICES, CROWS, LANES), F32),
            pltpu.SemaphoreType.DMA((2,)),
            pltpu.SemaphoreType.DMA((4,)),
            pltpu.SemaphoreType.DMA((4,)),
            pltpu.SemaphoreType.DMA((2 * REACH,)),
            pltpu.SemaphoreType.DMA((2 * REACH,)),
            pltpu.SemaphoreType.DMA((SLICES,)),
            pltpu.SemaphoreType.DMA((SLICES,)),
            pltpu.SemaphoreType.DMA((2 * REACH,)),
            pltpu.SemaphoreType.DMA((2 * REACH,)),
            pltpu.SemaphoreType.DMA((SLICES,)),
            pltpu.SemaphoreType.DMA((SLICES,)),
        ],
        compiler_params=pltpu.CompilerParams(
            collective_id=0, has_side_effects=True, vmem_limit_bytes=32 * 1024 * 1024
        ),
    )(tiled(states), tiled(stream))
    return ended.transpose(0, 2, 1, 3).reshape(1, BAND, COLS)


def solution(mesh):
    in_specs = (P("cuts", "space", None), P("space", None))
    out_specs = P("cuts", "space", None)
    return jax.shard_map(
        per_device, mesh=mesh, in_specs=in_specs, out_specs=out_specs, check_vma=False
    )
```

time: 537 us -> 61.6 us (0.11)
  the two profiles are of different devices: /device:TPU:64 before, /device:TPU:1 now
where the time goes in v1:
time: 61.6 us; the launch traced here: 61.5 us
  Pallas kernels  58.9 us (96%)
  local copies, waits for them, and re-layouts  2.6 us (4%)
    pallas_call x1, Pallas kernels, per_device(): pl.pallas_call(kernel, out_shape=jax.ShapeDtypeStruct((BAND // 8, FT, 8,...  58.9 us
    unnamed x5, local copies, waits for them, and re-layouts  2.6 us

profile of v1, /device:TPU:1, one launch (start us, length us, event | category | flops | bytes accessed | tf_op | source)
XLA Modules:
  0.0 61.5 jit_solution(5452792799025950841)
XLA Ops:
  0.0 0.0 copy-start
  0.0 0.9 %copy-done = f32[1,32,2048]{2,1,0:T(8,128)S(1)} copy-done((f32[1,32,2048]{2,1,0:T(8,128)S(1)}, f32[1,32,2048]{2,1,0:T(8,128)}, u32[]{:S(2)}) %copy-start) | copy-done | bytes 262168
  1.0 0.0 copy-start.1
  1.0 0.9 %copy-done.1 = f32[32,2048]{1,0:T(8,128)S(1)} copy-done((f32[32,2048]{1,0:T(8,128)S(1)}, f32[32,2048]{1,0:T(8,128)}, u32[]{:S(2)}) %copy-start.1) | copy-done | bytes 262168
  1.9 58.9 %shard_map.28 = f32[4,16,8,128]{3,2,1,0:T(8,128)S(1)} custom-call(f32[4,16,8,128]{3,2,1,0:T(8,128)S(1)} %bitcast.10, f32[4,16,8,128]{3,2,1,0:T(8,128)S(1)} %bitcast.11), custom_call_target="tpu_custom_call" | custom-call | tf_op jit(solution)/shard_map/pallas_call | solution.py:377
  60.8 0.7 %copy.4 = f32[1,32,2048]{2,1,0:T(8,128)} copy(f32[1,32,2048]{2,1,0:T(8,128)S(1)} %bitcast.9) | data formatting | bytes 524288
Async XLA Ops:
  0.0 0.9 %copy-start = (f32[1,32,2048]{2,1,0:T(8,128)S(1)}, f32[1,32,2048]{2,1,0:T(8,128)}, u32[]{:S(2)}) copy-start(f32[1,32,2048]{2,1,0:T(8,128)} %param.2) | copy-start | bytes 786436
  1.0 0.9 %copy-start.1 = (f32[32,2048]{1,0:T(8,128)S(1)}, f32[32,2048]{1,0:T(8,128)}, u32[]{:S(2)}) copy-start(f32[32,2048]{1,0:T(8,128)} %param.3) | copy-start | bytes 786436

commit v2 on v1

--- a/solution.py
+++ b/solution.py
@@ -215,16 +215,37 @@
         old = moved
 
     def fine_stage(s, src, dst):
-        def tile(c, carry):
-            t = src[c]
-            east, west = columns(src[lax.rem(c + FT - 1, FT)], t, src[lax.rem(c + 1, FT)])
-            change = operator(t, east, west, fce[c], fcw[c], fcn[c], fcs[c])
-            if s == 0:
-                change = FINE_START * change
-            dst[c] = FINE_BETAS[s] * base[c] + change
-            return carry
-
-        lax.fori_loop(0, FT, tile, 0)
+        lane = lax.broadcasted_iota(jnp.int32, (4, 8, LANES), 2)
+
+        def west_of(t):
+            return pltpu.roll(t, 1, 2)
+
+        def east_of(t):
+            return pltpu.roll(t, LANES - 1, 2)
+
+        for first in (0, 4):
+            part = pl.ds(first, 4)
+            west_before = west_of(src[FT - 1, part])
+            t = src[0, part]
+            east_now = east_of(t)
+            for c in range(FT):
+                after = src[(c + 1) % FT, part]
+                west_now, east_after = west_of(t), east_of(after)
+                west = jnp.where(lane == 0, west_before, west_now)
+                east = jnp.where(lane == LANES - 1, east_after, east_now)
+                if first == 0:
+                    up = jnp.concatenate([t[1:], src[c, pl.ds(4, 1)]], axis=0)
+                    down = jnp.concatenate([pltpu.roll(src[c, pl.ds(7, 1)], 1, 1), t[:-1]], axis=0)
+                else:
+                    up = jnp.concatenate([t[1:], pltpu.roll(src[c, pl.ds(0, 1)], 7, 1)], axis=0)
+                    down = jnp.concatenate([src[c, pl.ds(3, 1)], t[:-1]], axis=0)
+                change = (
+                    fce[c, part] * east + fcw[c, part] * west + fcn[c, part] * up + fcs[c, part] * down - t
+                )
+                if s == 0:
+                    change = FINE_START * change
+                dst[c, part] = FINE_BETAS[s] * base[c, part] + change
+                t, west_before, east_now = after, west_now, east_after
 
     def fine_step(step, carry):
         fine_stage(0, base, ta)
@@ -406,7 +427,7 @@
             pltpu.SemaphoreType.DMA((SLICES,)),
         ],
         compiler_params=pltpu.CompilerParams(
-            collective_id=0, has_side_effects=True, vmem_limit_bytes=32 * 1024 * 1024
+            collective_id=0, has_side_effects=True, vmem_limit_bytes=63 * 1024 * 1024
         ),
     )(tiled(states), tiled(stream))
     return ended.transpose(0, 2, 1, 3).reshape(1, BAND, COLS)

time: 61.6 us -> 39.1 us (0.63)
  Pallas kernels: 58.9 us -> 37.3 us
  local copies, waits for them, and re-layouts: 2.6 us -> 1.67 us
    pallas_call x1, Pallas kernels: 58.9 us -> 37.3 us  [per_device(): pl.pallas_call(kernel, out_shape=jax.ShapeDtypeStruct((BAND // 8, FT, 8,...]
    unnamed x5 -> x1, local copies, waits for them, and re-layouts: 2.6 us -> 1.67 us
where the time goes in v2:
time: 39.1 us; the launch traced here: 38.9 us
  Pallas kernels  37.3 us (95%)
  local copies, waits for them, and re-layouts  1.67 us (4%)
    pallas_call x1, Pallas kernels, per_device(): pl.pallas_call(kernel, out_shape=jax.ShapeDtypeStruct((BAND // 8, FT, 8,...  37.3 us
    unnamed x1, local copies, waits for them, and re-layouts  1.67 us

profile of v2, /device:TPU:1, one launch (start us, length us, event | category | flops | bytes accessed | tf_op | source)
XLA Modules:
  0.0 38.9 jit_solution(15143771877276476699)
XLA Ops:
  0.0 37.3 %shard_map.28 = f32[4,16,8,128]{3,2,1,0:T(8,128)} custom-call(f32[4,16,8,128]{3,2,1,0:T(8,128)} %bitcast.10, f32[4,16,8,128]{3,2,1,0:T(8,128)} %bitcast.11), custom_call_target="tpu_custom_call" | custom-call | tf_op jit(solution)/shard_map/pallas_call | solution.py:398
  37.3 1.7 %copy.4 = f32[1,32,2048]{2,1,0:T(8,128)} copy(f32[1,32,2048]{2,1,0:T(8,128)} %bitcast.9) | data formatting | bytes 524288

commit v3 on v2

--- a/solution.py
+++ b/solution.py
@@ -19,6 +19,7 @@
 CROWS = 8
 CWIDE = CROWS * (2 * REACH + 1)
 FINE_STEPS = 4
+GROUP = 4
 F32 = jnp.float32
 
 
@@ -60,19 +61,36 @@
 
 
 def matmul(x, m):
-    return jnp.dot(x, m, precision=lax.Precision.HIGHEST, preferred_element_type=F32)
+    high = x.astype(jnp.bfloat16)
+    x = x - high.astype(F32)
+    middle = x.astype(jnp.bfloat16)
+    low = (x - middle.astype(F32)).astype(jnp.bfloat16)
+    small = jnp.dot(low, m, preferred_element_type=F32) + jnp.dot(middle, m, preferred_element_type=F32)
+    return jnp.dot(high, m, preferred_element_type=F32) + small
 
 
 def kernel(
     states, stream, out,
-    xwin, swin, base, ta, tb, fce, fcw, fcn, fcs, shrink, grow, rows, cbuf, wstream, wgap, spw, pay, nbuf, newc,
+    xwin, swin, base, ta, tb, fce, fcw, fcn, fcs, shrink, grow, rows, cbuf, wstream, wgap, spw, pay, nbuf, newc, spread_rows,
     local_sem, halo_send, halo_recv, sc_send, sc_recv, a_send, a_recv, b_send, b_recv, c_send, c_recv,
 ):
     n = lax.axis_index("cuts")
     b = lax.axis_index("space")
 
+    def flipped(k, bit):
+        return k + bit * (1 - 2 * lax.rem(k, 2))
+
+    side = lax.rem(b // 2, 2)
+    column = flipped(n, side)
+
     def at_space(j):
         return (n, lax.rem(b + (SPACE + j), SPACE))
+
+    def at_window(j):
+        other = lax.rem(b + (SPACE + j), SPACE)
+        return (flipped(n, lax.rem(side + lax.rem(other // 2, 2), 2)), other)
+
+    across = 2 * lax.rem(b, 2) - 1
 
     offsets = [j for d in range(1, REACH + 1) for j in (-d, d)]
 
@@ -87,24 +105,23 @@
     newc[...] = jnp.zeros_like(newc)
 
     barrier = pltpu.get_barrier_semaphore()
-    for j in offsets:
-        pl.semaphore_signal(barrier, inc=1, device_id=at_space(j), device_id_type=MESH)
-    for k in range(1, SLICES):
-        pl.semaphore_signal(
-            barrier, inc=1, device_id=(lax.rem(n + k, SLICES), b), device_id_type=MESH
-        )
-    pl.semaphore_wait(barrier, len(offsets) + SLICES - 1)
+    greeted = [at_space(across)]
+    greeted += [(lax.rem(n + k, SLICES), b) for k in range(1, SLICES)]
+    greeted += [at_window(j) for j in reversed(offsets)]
+    for device in greeted:
+        pl.semaphore_signal(barrier, inc=1, device_id=device, device_id_type=MESH)
+    pl.semaphore_wait(barrier, len(greeted))
 
     halos = []
-    for at, (source, window) in enumerate(((stream, swin), (states, xwin))):
-        for side, (j, first, target) in enumerate(((1, BAND - HALO, 0), (-1, 0, HALO + BAND))):
+    for at, (source, window, device) in enumerate(((stream, swin, at_window), (states, xwin, at_space))):
+        for end, (j, first, target) in enumerate(((1, BAND - HALO, 0), (-1, 0, HALO + BAND))):
             halos.append(
                 pltpu.make_async_remote_copy(
                     src_ref=source.at[pl.ds(first // 8, HALO // 8)],
                     dst_ref=window.at[pl.ds(target // 8, HALO // 8)],
-                    send_sem=halo_send.at[2 * at + side],
-                    recv_sem=halo_recv.at[2 * at + side],
-                    device_id=at_space(j),
+                    send_sem=halo_send.at[2 * at + end],
+                    recv_sem=halo_recv.at[2 * at + end],
+                    device_id=device(j),
                     device_id_type=MESH,
                 )
             )
@@ -112,10 +129,10 @@
 
     fine_at = lax.broadcasted_iota(jnp.int32, (4 * LANES, LANES), 0)
     coarse_at = lax.broadcasted_iota(jnp.int32, (4 * LANES, LANES), 1)
-    shrink[...] = jnp.where((fine_at >> 2) == coarse_at, 0.0625, 0.0).astype(F32)
+    shrink[...] = jnp.where((fine_at >> 2) == coarse_at, 0.0625, 0.0).astype(jnp.bfloat16)
     fine_at = lax.broadcasted_iota(jnp.int32, (LANES, 4 * LANES), 1)
     coarse_at = lax.broadcasted_iota(jnp.int32, (LANES, 4 * LANES), 0)
-    grow[...] = jnp.where((fine_at >> 2) == coarse_at, 1.0, 0.0).astype(F32)
+    grow[...] = jnp.where((fine_at >> 2) == coarse_at, 1.0, 0.0).astype(jnp.bfloat16)
 
     def windows(tiles, target):
         lane = lax.broadcasted_iota(jnp.int32, (CROWS, LANES), 1)
@@ -140,16 +157,16 @@
     for at, j in enumerate(offsets):
         spreads.append(
             pltpu.make_async_remote_copy(
-                src_ref=wstream.at[n],
+                src_ref=wstream.at[column],
                 dst_ref=spw.at[pl.ds(CROWS * (REACH - j), CROWS)],
                 send_sem=sc_send.at[at],
                 recv_sem=sc_recv.at[at],
-                device_id=at_space(j),
+                device_id=at_window(j),
                 device_id_type=MESH,
             )
         )
         spreads[-1].start()
-    spw[pl.ds(CROWS * REACH, CROWS)] = wstream[n]
+    spw[pl.ds(CROWS * REACH, CROWS)] = wstream[column]
     own_x.wait()
 
     for halo in halos[:2]:
@@ -160,49 +177,52 @@
             [window[pl.ds(c * 8 + r, 8, stride=FT * 8)] for r in range(8)]
         )
 
-    def weights(c, carry):
-        psi = window_tile(srows, c)
-        east, west = columns(
-            window_tile(srows, lax.rem(c + FT - 1, FT)), psi, window_tile(srows, lax.rem(c + 1, FT))
-        )
-        ce, cn = coefficients(psi, east, west)
+    def add_rows(c, t):
+        for q in range(2):
+            rows[pl.ds(8 * (2 * (c // 4) + q), 8), pl.ds(c % 4 * LANES, LANES)] = (
+                t[4 * q] + t[4 * q + 1] + (t[4 * q + 2] + t[4 * q + 3])
+            )
+
+    def restricted():
+        small = matmul(rows[...], shrink[...])
+        return [
+            jnp.stack([small[8 * (2 * c + q):8 * (2 * c + q + 1)] for q in range(2)]) for c in range(CT)
+        ]
+
+    lane = lax.broadcasted_iota(jnp.int32, (8, 8, LANES), 2)
+    west_before = pltpu.roll(window_tile(srows, FT - 1), 1, 2)
+    psi = window_tile(srows, 0)
+    east_now = pltpu.roll(psi, LANES - 1, 2)
+    for c in range(FT):
+        after = window_tile(srows, (c + 1) % FT)
+        west_now, east_after = pltpu.roll(psi, 1, 2), pltpu.roll(after, LANES - 1, 2)
+        ce, cn = coefficients(
+            psi,
+            jnp.where(lane == LANES - 1, east_after, east_now),
+            jnp.where(lane == 0, west_before, west_now),
+        )
         fce[c] = ce
         fcw[c] = 0.5 - ce
         fcn[c] = cn
         fcs[c] = 0.5 - cn
-        return carry
-
-    lax.fori_loop(0, FT, weights, 0)
-
-    for halo in halos[2:]:
-        halo.wait_recv()
-
-    def begin(c, carry):
-        base[c] = window_tile(xrows, c)
-        return carry
-
-    lax.fori_loop(0, FT, begin, 0)
-
-    def restrict(tile):
-        for c in range(CT):
-            for m in range(4):
-                t = tile(4 * c + m)
-                for q in range(2):
-                    rows[pl.ds(8 * (2 * c + q), 8), pl.ds(m * LANES, LANES)] = (
-                        t[4 * q] + t[4 * q + 1] + t[4 * q + 2] + t[4 * q + 3]
-                    )
-        small = matmul(rows[...], shrink[...])
-        return [
-            jnp.stack([small[8 * (2 * c + q):8 * (2 * c + q + 1)] for q in range(2)]) for c in range(CT)
-        ]
-
-    cpsi = restrict(lambda c: window_tile(srows, c))
+        add_rows(c, psi)
+        psi, west_before, east_now = after, west_now, east_after
+
+    cpsi = restricted()
     cweights = []
     for c in range(CT):
         east, west = columns(cpsi[c - 1], cpsi[c], cpsi[(c + 1) % CT])
         ce, cn = coefficients(cpsi[c], east, west)
         cweights.append((ce, 0.5 - ce, cn, 0.5 - cn))
-    start = restrict(lambda c: base[c])
+
+    for halo in halos[2:]:
+        halo.wait_recv()
+    for c in range(FT):
+        t = window_tile(xrows, c)
+        base[c] = t
+        add_rows(c, t)
+
+    start = restricted()
     old = start
     for s in range(4):
         moved = []
@@ -215,7 +235,7 @@
         old = moved
 
     def fine_stage(s, src, dst):
-        lane = lax.broadcasted_iota(jnp.int32, (4, 8, LANES), 2)
+        lane = lax.broadcasted_iota(jnp.int32, (GROUP, 8, LANES), 2)
 
         def west_of(t):
             return pltpu.roll(t, 1, 2)
@@ -223,8 +243,8 @@
         def east_of(t):
             return pltpu.roll(t, LANES - 1, 2)
 
-        for first in (0, 4):
-            part = pl.ds(first, 4)
+        for first in range(0, 8, GROUP):
+            part = pl.ds(first, GROUP)
             west_before = west_of(src[FT - 1, part])
             t = src[0, part]
             east_now = east_of(t)
@@ -233,14 +253,18 @@
                 west_now, east_after = west_of(t), east_of(after)
                 west = jnp.where(lane == 0, west_before, west_now)
                 east = jnp.where(lane == LANES - 1, east_after, east_now)
-                if first == 0:
-                    up = jnp.concatenate([t[1:], src[c, pl.ds(4, 1)]], axis=0)
-                    down = jnp.concatenate([pltpu.roll(src[c, pl.ds(7, 1)], 1, 1), t[:-1]], axis=0)
+                if first + GROUP < 8:
+                    above = src[c, pl.ds(first + GROUP, 1)]
                 else:
-                    up = jnp.concatenate([t[1:], pltpu.roll(src[c, pl.ds(0, 1)], 7, 1)], axis=0)
-                    down = jnp.concatenate([src[c, pl.ds(3, 1)], t[:-1]], axis=0)
-                change = (
-                    fce[c, part] * east + fcw[c, part] * west + fcn[c, part] * up + fcs[c, part] * down - t
+                    above = pltpu.roll(src[c, pl.ds(0, 1)], 7, 1)
+                if first > 0:
+                    below = src[c, pl.ds(first - 1, 1)]
+                else:
+                    below = pltpu.roll(src[c, pl.ds(7, 1)], 1, 1)
+                up = jnp.concatenate([t[1:], above], axis=0)
+                down = jnp.concatenate([below, t[:-1]], axis=0)
+                change = (fcn[c, part] * up + fcs[c, part] * down - t) + (
+                    fce[c, part] * east + fcw[c, part] * west
                 )
                 if s == 0:
                     change = FINE_START * change
@@ -256,7 +280,9 @@
 
     lax.fori_loop(0, FINE_STEPS, fine_step, 0)
 
-    ended = restrict(lambda c: base[c])
+    for c in range(FT):
+        add_rows(c, base[c])
+    ended = restricted()
     gap = [ended[c] - old[c] for c in range(CT)]
     gap = [jnp.where(n == 0, old[c] + gap[c], gap[c]) for c in range(CT)]
     for c in range(CT):
@@ -268,7 +294,7 @@
 
     def gap_copy(k, m):
         return pltpu.make_async_remote_copy(
-            src_ref=wgap.at[k],
+            src_ref=wgap.at[flipped(k, side)],
             dst_ref=pay.at[m, middle],
             send_sem=a_send.at[k],
             recv_sem=a_recv.at[m],
@@ -283,7 +309,7 @@
 
     @pl.when(n < SLICES - 1)
     def _():
-        pay[n, middle] = wgap[n]
+        pay[n, middle] = wgap[column]
 
     for spread in spreads:
         spread.wait()
@@ -305,20 +331,29 @@
                 dst_ref=pay.at[pl.ds(0, count), pl.ds(CROWS * (REACH - j), CROWS)],
                 send_sem=b_send.at[at],
                 recv_sem=b_recv.at[at],
-                device_id=at_space(j),
+                device_id=at_window(j),
                 device_id_type=MESH,
             )
         )
         gathers[-1].start()
+
+    for c in range(FT):
+        t = base[c]
+        for r in range(8):
+            xrows[pl.ds(c * 8 + r, 8, stride=FT * 8)] = t[r]
+    for c in range(CT):
+        for q in range(2):
+            cbuf[c, pl.ds(4 + q, 8, stride=2)] = old[c][q]
+
     for gather in gathers:
         gather.wait_recv()
 
-    def new_copy(i, k):
+    def new_copy(i, window):
         return pltpu.make_async_remote_copy(
             src_ref=nbuf.at[i, middle],
-            dst_ref=newc.at[k],
+            dst_ref=newc.at[window],
             send_sem=c_send.at[i],
-            recv_sem=c_recv.at[k],
+            recv_sem=c_recv.at[window],
             device_id=(i, b),
             device_id_type=MESH,
         )
@@ -335,11 +370,11 @@
 
         @pl.when(i != n)
         def _():
-            new_copy(i, n).start()
+            new_copy(i, column).start()
 
         @pl.when(i == n)
         def _():
-            newc[n] = nbuf[i, middle]
+            newc[column] = nbuf[i, middle]
 
         late = lax.rem(i, SLICES - 1)
         return t + jnp.stack([pay[late, pl.ds(4 + r, 8, stride=8)] for r in range(8)])
@@ -350,29 +385,25 @@
     for k in range(SLICES):
         @pl.when((n != k) & (n > 0))
         def _():
-            new_copy(k, k).wait_recv()
+            new_copy(k, flipped(k, side)).wait_recv()
 
     lane = lax.broadcasted_iota(jnp.int32, (CROWS, LANES), 1)
     for c in range(CT):
-        cbuf[c, pl.ds(8, CROWS)] = jnp.where(
+        new = jnp.where(
             lane < LANES // 2, pltpu.roll(newc[2 * c], LANES - 32, 1), pltpu.roll(newc[2 * c + 1], 32, 1)
         )
-    parts = []
-    for c in range(CT):
-        for q in range(2):
-            new = cbuf[c, pl.ds(4 + q, 8, stride=2)]
-            new = jnp.where(n == 0, old[c][q], new)
-            parts.append(new - old[c][q])
-    rows[...] = matmul(jnp.concatenate(parts, axis=0), grow[...])
+        was = cbuf[c, pl.ds(8, CROWS)]
+        change = jnp.where(n == 0, was, new) - was
+        for i in range(4):
+            spread_rows[pl.ds(BAND * c + i, CROWS, stride=4)] = change
+    fine_change = matmul(spread_rows[...], grow[...])
     for c in range(CT):
         for m in range(4):
-            t = base[4 * c + m]
-            for r in range(8):
-                xrows[pl.ds((4 * c + m) * 8 + r, 8, stride=FT * 8)] = (
-                    t[r] + rows[pl.ds(8 * (2 * c + r // 4), 8), pl.ds(m * LANES, LANES)]
+            for i in range(BAND // 8):
+                out[i, 4 * c + m] = (
+                    xwin[HALO // 8 + i, 4 * c + m]
+                    + fine_change[BAND * c + 8 * i:BAND * c + 8 * (i + 1), m * LANES:(m + 1) * LANES]
                 )
-    result = pltpu.make_async_copy(xwin.at[pl.ds(HALO // 8, BAND // 8)], out, local_sem.at[0])
-    result.start()
 
     for halo in halos:
         halo.wait_send()
@@ -385,8 +416,7 @@
     for i in range(1, SLICES):
         @pl.when(n != i)
         def _():
-            new_copy(i, n).wait_send()
-    result.wait()
+            new_copy(i, column).wait_send()
 
 
 def per_device(states, stream):
@@ -397,15 +427,15 @@
 
     ended = pl.pallas_call(
         kernel,
-        out_shape=jax.ShapeDtypeStruct((BAND // 8, FT, 8, LANES), F32),
+        out_shape=pltpu.VMEM((BAND // 8, FT, 8, LANES), F32),
         in_specs=[pl.BlockSpec(memory_space=pl.ANY)] * 2,
-        out_specs=pl.BlockSpec(memory_space=pl.ANY),
+        out_specs=pl.BlockSpec(memory_space=pltpu.VMEM),
         scratch_shapes=[
             pltpu.VMEM((WIDE // 8, FT, 8, LANES), F32),
             pltpu.VMEM((WIDE // 8, FT, 8, LANES), F32),
             tiles, tiles, tiles, tiles, tiles, tiles, tiles,
-            pltpu.VMEM((4 * LANES, LANES), F32),
-            pltpu.VMEM((LANES, 4 * LANES), F32),
+            pltpu.VMEM((4 * LANES, LANES), jnp.bfloat16),
+            pltpu.VMEM((LANES, 4 * LANES), jnp.bfloat16),
             pltpu.VMEM((2 * CT * 8, 4 * LANES), F32),
             pltpu.VMEM((CT, 24, LANES), F32),
             pltpu.VMEM((SLICES, CROWS, LANES), F32),
@@ -414,6 +444,7 @@
             pltpu.VMEM((SLICES - 1, CWIDE, LANES), F32),
             pltpu.VMEM((SLICES, CWIDE, LANES), F32),
             pltpu.VMEM((SLICES, CROWS, LANES), F32),
+            pltpu.VMEM((CT * BAND, LANES), F32),
             pltpu.SemaphoreType.DMA((2,)),
             pltpu.SemaphoreType.DMA((4,)),
             pltpu.SemaphoreType.DMA((4,)),
@@ -427,7 +458,7 @@
             pltpu.SemaphoreType.DMA((SLICES,)),
         ],
         compiler_params=pltpu.CompilerParams(
-            collective_id=0, has_side_effects=True, vmem_limit_bytes=63 * 1024 * 1024
+            collective_id=0, has_side_effects=True, vmem_limit_bytes=60 * 1024 * 1024
         ),
     )(tiled(states), tiled(stream))
     return ended.transpose(0, 2, 1, 3).reshape(1, BAND, COLS)

time: 39.1 us -> 36.8 us (0.941)
  Pallas kernels: 37.3 us -> 36 us
  local copies, waits for them, and re-layouts: 1.67 us -> 0.71 us
    pallas_call x1, Pallas kernels: 37.3 us -> 36 us  [per_device(): pl.pallas_call(kernel, out_shape=pltpu.VMEM((BAND // 8, FT, 8, LANES), F3...]
    unnamed x1, local copies, waits for them, and re-layouts: 1.67 us -> 0.71 us
where the time goes in v3:
time: 36.8 us; the launch traced here: 36.7 us
  Pallas kernels  36 us (98%)
  local copies, waits for them, and re-layouts  0.71 us (2%)
    pallas_call x1, Pallas kernels, per_device(): pl.pallas_call(kernel, out_shape=pltpu.VMEM((BAND // 8, FT, 8, LANES), F3...  36 us

profile of v3, /device:TPU:1, one launch (start us, length us, event | category | flops | bytes accessed | tf_op | source)
XLA Modules:
  0.0 36.7 jit_solution(12849019866325205803)
XLA Ops:
  0.0 36.0 %shard_map.28 = f32[4,16,8,128]{3,2,1,0:T(8,128)S(1)} custom-call(f32[4,16,8,128]{3,2,1,0:T(8,128)} %bitcast.10, f32[4,16,8,128]{3,2,1,0:T(8,128)} %bitcast.11), custom_call_target="tpu_custom_call" | custom-call | tf_op jit(solution)/shard_map/pallas_call | solution.py:428
  36.0 0.7 %copy.4 = f32[1,32,2048]{2,1,0:T(8,128)} copy(f32[1,32,2048]{2,1,0:T(8,128)S(1)} %bitcast.9) | data formatting | bytes 524288

commit v4 on v3

--- a/solution.py
+++ b/solution.py
@@ -19,7 +19,8 @@
 CROWS = 8
 CWIDE = CROWS * (2 * REACH + 1)
 FINE_STEPS = 4
-GROUP = 4
+SPAN = 4
+STAGES = 4 * FINE_STEPS
 F32 = jnp.float32
 
 
@@ -41,13 +42,6 @@
 
 def rows_down(t):
     return jnp.concatenate([pltpu.roll(t[-1:], 1, 1), t[:-1]], axis=0)
-
-
-def columns(left, t, right):
-    lane = lax.broadcasted_iota(jnp.int32, t.shape, 2)
-    west = jnp.where(lane == 0, pltpu.roll(left, 1, 2), pltpu.roll(t, 1, 2))
-    east = jnp.where(lane == LANES - 1, pltpu.roll(right, LANES - 1, 2), pltpu.roll(t, LANES - 1, 2))
-    return east, west
 
 
 def coefficients(psi, east, west):
@@ -71,7 +65,7 @@
 
 def kernel(
     states, stream, out,
-    xwin, swin, base, ta, tb, fce, fcw, fcn, fcs, shrink, grow, rows, cbuf, wstream, wgap, spw, pay, nbuf, newc, spread_rows,
+    xwin, swin, psi, field, fce, fcn, shrink, grow, rows, cpsi, cce, ccn, cfield, wstream, wgap, spw, pay, nbuf, newc, spread_rows,
     local_sem, halo_send, halo_recv, sc_send, sc_recv, a_send, a_recv, b_send, b_recv, c_send, c_recv,
 ):
     n = lax.axis_index("cuts")
@@ -96,8 +90,6 @@
 
     own_x = pltpu.make_async_copy(states, xwin.at[pl.ds(HALO // 8, BAND // 8)], local_sem.at[0])
     own_s = pltpu.make_async_copy(stream, swin.at[pl.ds(HALO // 8, BAND // 8)], local_sem.at[1])
-    xrows = xwin.reshape(WIDE * FT, LANES)
-    srows = swin.reshape(WIDE * FT, LANES)
     own_s.start()
     own_x.start()
 
@@ -142,17 +134,34 @@
             target[2 * j] = jnp.where(lane < 32, right[(j - 1) % CT], right[j])
             target[2 * j + 1] = jnp.where(lane < LANES - 32, left[j], left[(j + 1) % CT])
 
+    own = range(HALO // 8, (HALO + BAND) // 8)
+    around = [i for i in range(WIDE // 8) if i not in own]
+
+    def untile(window, target, parts):
+        for i in parts:
+            for c in range(FT):
+                target[c, pl.ds(8 * i, 8)] = window[i, c]
+
+    def add_rows(source, at, first):
+        for c in range(FT):
+            parts = [source[c, pl.ds(first + i, 8, stride=4)] for i in range(4)]
+            rows[pl.ds(at(c // 4), 8), pl.ds(c % 4 * LANES, LANES)] = parts[0] + parts[1] + (parts[2] + parts[3])
+
+    def restricted_band(source):
+        add_rows(source, lambda c: CROWS * c, HALO)
+        small = matmul(rows[pl.ds(0, CROWS * CT)], shrink[...])
+        return [small[CROWS * c:CROWS * (c + 1)] for c in range(CT)]
+
+    def restricted_window(source, target):
+        for half in range(2):
+            add_rows(source, lambda c: 2 * CROWS * c + CROWS * half, half * WIDE // 2)
+        small = matmul(rows[...], shrink[...])
+        for c in range(CT):
+            target[c] = small[2 * CROWS * c:2 * CROWS * (c + 1)]
+
     own_s.wait()
-    for c in range(CT):
-        for m in range(4):
-            for half in range(2):
-                parts = [srows[pl.ds(2 * FT * 8 + (4 * c + m) * 8 + 4 * half + i, 4, stride=FT * 8)] for i in range(4)]
-                rows[pl.ds(8 * c + 4 * half, 4), pl.ds(m * LANES, LANES)] = parts[0] + parts[1] + parts[2] + parts[3]
-    small = matmul(rows[pl.ds(0, CROWS * CT)], shrink[...])
-    for c in range(CT):
-        for half in range(2):
-            cbuf[c, pl.ds(half, 4, stride=2)] = small[8 * c + 4 * half:8 * c + 4 * half + 4]
-    windows([cbuf[c, pl.ds(0, CROWS)] for c in range(CT)], wstream)
+    untile(swin, psi, own)
+    windows(restricted_band(psi), wstream)
     spreads = []
     for at, j in enumerate(offsets):
         spreads.append(
@@ -169,126 +178,115 @@
     spw[pl.ds(CROWS * REACH, CROWS)] = wstream[column]
     own_x.wait()
 
+    def first_lane(t):
+        return lax.broadcasted_iota(jnp.int32, t.shape, 1) == 0
+
+    def last_lane(t):
+        return lax.broadcasted_iota(jnp.int32, t.shape, 1) == LANES - 1
+
+    def wrapped(c):
+        return c % FT if isinstance(c, int) else lax.rem(c, FT)
+
+    def over_tiles(source, blocks, tiles, work):
+        def west_of(c):
+            return [pltpu.roll(source[c, pl.ds(*block)], 1, 1) for block in blocks]
+
+        def east_of(c):
+            return [pltpu.roll(source[c, pl.ds(*block)], LANES - 1, 1) for block in blocks]
+
+        before, now = west_of(wrapped(tiles[0] + FT - 1)), east_of(tiles[0])
+        for c in tiles:
+            west_now, after = west_of(c), east_of(wrapped(c + 1))
+            for i, block in enumerate(blocks):
+                t = source[c, pl.ds(*block)]
+                west = jnp.where(first_lane(t), before[i], west_now[i])
+                east = jnp.where(last_lane(t), after[i], now[i])
+                work(c, block, t, east, west)
+            before, now = west_now, after
+
+    def shifted(source, c, block, by):
+        return source[c, pl.ds(block[0] + by, block[1])]
+
+    def weigh(c, block, t, east, west):
+        fce[c, pl.ds(*block)] = 0.25 - 0.3125 * (shifted(psi, c, block, 1) - shifted(psi, c, block, -1))
+        fcn[c, pl.ds(*block)] = 0.25 + 0.3125 * (east - west)
+
+    def stage(at, base_at, s, blocks, tiles):
+        source, base, target = field.at[at], field.at[base_at], field.at[at + 1]
+
+        def work(c, block, t, east, west):
+            here = pl.ds(*block)
+            up, down = shifted(source, c, block, 1), shifted(source, c, block, -1)
+            change = fcn[c, here] * (up - down) + (0.5 * (west + down) - t) + fce[c, here] * (east - west)
+            if s == 0:
+                change = FINE_START * change
+            target[c, here] = FINE_BETAS[s] * base[c, here] + change
+
+        over_tiles(source, blocks, tiles, work)
+
+    def blocks_of(first, last):
+        count = max((last - first + 7) // 8, 1)
+        return [(first + 8 * i, 8) for i in range(count - 1)] + [(max(last - 8, first), 8)]
+
+    def by_runs(work):
+        def run(at, carry):
+            work([at * SPAN + i for i in range(SPAN)])
+            return carry
+
+        lax.fori_loop(0, FT // SPAN, run, 0)
+
+    untile(xwin, field.at[0], own)
+    by_runs(lambda tiles: over_tiles(psi, blocks_of(HALO + 1, HALO + BAND - 1), tiles, weigh))
+    for k in range(STAGES - 1):
+        inner = blocks_of(HALO + k + 1, HALO + BAND - k - 1)
+        by_runs(lambda tiles: stage(k, k // 4 * 4, k % 4, inner, tiles))
+
     for halo in halos[:2]:
         halo.wait_recv()
-
-    def window_tile(window, c):
-        return jnp.stack(
-            [window[pl.ds(c * 8 + r, 8, stride=FT * 8)] for r in range(8)]
-        )
-
-    def add_rows(c, t):
-        for q in range(2):
-            rows[pl.ds(8 * (2 * (c // 4) + q), 8), pl.ds(c % 4 * LANES, LANES)] = (
-                t[4 * q] + t[4 * q + 1] + (t[4 * q + 2] + t[4 * q + 3])
-            )
-
-    def restricted():
-        small = matmul(rows[...], shrink[...])
-        return [
-            jnp.stack([small[8 * (2 * c + q):8 * (2 * c + q + 1)] for q in range(2)]) for c in range(CT)
-        ]
-
-    lane = lax.broadcasted_iota(jnp.int32, (8, 8, LANES), 2)
-    west_before = pltpu.roll(window_tile(srows, FT - 1), 1, 2)
-    psi = window_tile(srows, 0)
-    east_now = pltpu.roll(psi, LANES - 1, 2)
-    for c in range(FT):
-        after = window_tile(srows, (c + 1) % FT)
-        west_now, east_after = pltpu.roll(psi, 1, 2), pltpu.roll(after, LANES - 1, 2)
-        ce, cn = coefficients(
-            psi,
-            jnp.where(lane == LANES - 1, east_after, east_now),
-            jnp.where(lane == 0, west_before, west_now),
-        )
-        fce[c] = ce
-        fcw[c] = 0.5 - ce
-        fcn[c] = cn
-        fcs[c] = 0.5 - cn
-        add_rows(c, psi)
-        psi, west_before, east_now = after, west_now, east_after
-
-    cpsi = restricted()
-    cweights = []
+    untile(swin, psi, around)
+    over_tiles(psi, [(1, HALO), (WIDE - 1 - HALO, HALO)], range(FT), weigh)
+    restricted_window(psi, cpsi)
+    middle_rows = [(1, 8), (7, 8)]
     for c in range(CT):
-        east, west = columns(cpsi[c - 1], cpsi[c], cpsi[(c + 1) % CT])
-        ce, cn = coefficients(cpsi[c], east, west)
-        cweights.append((ce, 0.5 - ce, cn, 0.5 - cn))
+        for block in middle_rows:
+            t = [cpsi[(c + d) % CT, pl.ds(*block)] for d in (-1, 0, 1)]
+            west = jnp.where(first_lane(t[1]), pltpu.roll(t[0], 1, 1), pltpu.roll(t[1], 1, 1))
+            east = jnp.where(last_lane(t[1]), pltpu.roll(t[2], LANES - 1, 1), pltpu.roll(t[1], LANES - 1, 1))
+            cce[c, pl.ds(*block)] = 0.25 - 0.3125 * (shifted(cpsi, c, block, 1) - shifted(cpsi, c, block, -1))
+            ccn[c, pl.ds(*block)] = 0.25 + 0.3125 * (east - west)
 
     for halo in halos[2:]:
         halo.wait_recv()
-    for c in range(FT):
-        t = window_tile(xrows, c)
-        base[c] = t
-        add_rows(c, t)
-
-    start = restricted()
-    old = start
+    untile(xwin, field.at[0], around)
+
+    restricted_window(field.at[0], cfield.at[0])
     for s in range(4):
-        moved = []
         for c in range(CT):
-            east, west = columns(old[c - 1], old[c], old[(c + 1) % CT])
-            change = operator(old[c], east, west, *cweights[c])
-            if s == 0:
-                change = COARSE_START * change
-            moved.append(COARSE_BETAS[s] * start[c] + change)
-        old = moved
-
-    def fine_stage(s, src, dst):
-        lane = lax.broadcasted_iota(jnp.int32, (GROUP, 8, LANES), 2)
-
-        def west_of(t):
-            return pltpu.roll(t, 1, 2)
-
-        def east_of(t):
-            return pltpu.roll(t, LANES - 1, 2)
-
-        for first in range(0, 8, GROUP):
-            part = pl.ds(first, GROUP)
-            west_before = west_of(src[FT - 1, part])
-            t = src[0, part]
-            east_now = east_of(t)
-            for c in range(FT):
-                after = src[(c + 1) % FT, part]
-                west_now, east_after = west_of(t), east_of(after)
-                west = jnp.where(lane == 0, west_before, west_now)
-                east = jnp.where(lane == LANES - 1, east_after, east_now)
-                if first + GROUP < 8:
-                    above = src[c, pl.ds(first + GROUP, 1)]
-                else:
-                    above = pltpu.roll(src[c, pl.ds(0, 1)], 7, 1)
-                if first > 0:
-                    below = src[c, pl.ds(first - 1, 1)]
-                else:
-                    below = pltpu.roll(src[c, pl.ds(7, 1)], 1, 1)
-                up = jnp.concatenate([t[1:], above], axis=0)
-                down = jnp.concatenate([below, t[:-1]], axis=0)
-                change = (fcn[c, part] * up + fcs[c, part] * down - t) + (
-                    fce[c, part] * east + fcw[c, part] * west
-                )
+            for block in [(s + 1, 8), (7 - s, 8)][:2 if s < 3 else 1]:
+                here = pl.ds(*block)
+                t = [cfield[s, (c + d) % CT, here] for d in (-1, 0, 1)]
+                west = jnp.where(first_lane(t[1]), pltpu.roll(t[0], 1, 1), pltpu.roll(t[1], 1, 1))
+                east = jnp.where(last_lane(t[1]), pltpu.roll(t[2], LANES - 1, 1), pltpu.roll(t[1], LANES - 1, 1))
+                up, down = shifted(cfield.at[s], c, block, 1), shifted(cfield.at[s], c, block, -1)
+                change = ccn[c, here] * (up - down) + (0.5 * (west + down) - t[1]) + cce[c, here] * (east - west)
                 if s == 0:
-                    change = FINE_START * change
-                dst[c, part] = FINE_BETAS[s] * base[c, part] + change
-                t, west_before, east_now = after, west_now, east_after
+                    change = COARSE_START * change
+                cfield[s + 1, c, here] = COARSE_BETAS[s] * cfield[0, c, here] + change
+    coarse_old = [cfield.at[4, c, pl.ds(4, CROWS)] for c in range(CT)]
 
     def fine_step(step, carry):
-        fine_stage(0, base, ta)
-        fine_stage(1, ta, tb)
-        fine_stage(2, tb, ta)
-        fine_stage(3, ta, base)
+        for s in range(4):
+            done = 4 * step + s
+            blocks = [(done + 1, HALO), (WIDE - HALO - 1 - done, HALO)]
+            stage(done, 4 * step, s, blocks, range(FT))
         return carry
 
     lax.fori_loop(0, FINE_STEPS, fine_step, 0)
-
-    for c in range(FT):
-        add_rows(c, base[c])
-    ended = restricted()
-    gap = [ended[c] - old[c] for c in range(CT)]
-    gap = [jnp.where(n == 0, old[c] + gap[c], gap[c]) for c in range(CT)]
-    for c in range(CT):
-        for q in range(2):
-            cbuf[c, pl.ds(4 + q, 8, stride=2)] = gap[c][q]
-    windows([cbuf[c, pl.ds(8, CROWS)] for c in range(CT)], wgap)
+    fine_end = field.at[STAGES]
+
+    ended = restricted_band(fine_end)
+    gap = [ended[c] - coarse_old[c][...] for c in range(CT)]
+    windows([jnp.where(n == 0, coarse_old[c][...] + gap[c], gap[c]) for c in range(CT)], wgap)
 
     middle = pl.ds(CROWS * REACH, CROWS)
 
@@ -313,8 +311,10 @@
 
     for spread in spreads:
         spread.wait()
-    psi = jnp.stack([spw[pl.ds(4 + r, 8, stride=8)] for r in range(8)])
-    ce, cn = coefficients(psi, pltpu.roll(psi, LANES - 1, 2), pltpu.roll(psi, 1, 2))
+    around_psi = jnp.stack([spw[pl.ds(4 + r, 8, stride=8)] for r in range(8)])
+    ce, cn = coefficients(
+        around_psi, pltpu.roll(around_psi, LANES - 1, 2), pltpu.roll(around_psi, 1, 2)
+    )
     chain_weights = (ce, 0.5 - ce, cn, 0.5 - cn)
 
     for m in range(SLICES - 1):
@@ -337,14 +337,6 @@
         )
         gathers[-1].start()
 
-    for c in range(FT):
-        t = base[c]
-        for r in range(8):
-            xrows[pl.ds(c * 8 + r, 8, stride=FT * 8)] = t[r]
-    for c in range(CT):
-        for q in range(2):
-            cbuf[c, pl.ds(4 + q, 8, stride=2)] = old[c][q]
-
     for gather in gathers:
         gather.wait_recv()
 
@@ -392,7 +384,7 @@
         new = jnp.where(
             lane < LANES // 2, pltpu.roll(newc[2 * c], LANES - 32, 1), pltpu.roll(newc[2 * c + 1], 32, 1)
         )
-        was = cbuf[c, pl.ds(8, CROWS)]
+        was = coarse_old[c][...]
         change = jnp.where(n == 0, was, new) - was
         for i in range(4):
             spread_rows[pl.ds(BAND * c + i, CROWS, stride=4)] = change
@@ -401,7 +393,7 @@
         for m in range(4):
             for i in range(BAND // 8):
                 out[i, 4 * c + m] = (
-                    xwin[HALO // 8 + i, 4 * c + m]
+                    fine_end[4 * c + m, pl.ds(HALO + 8 * i, 8)]
                     + fine_change[BAND * c + 8 * i:BAND * c + 8 * (i + 1), m * LANES:(m + 1) * LANES]
                 )
 
@@ -420,7 +412,8 @@
 
 
 def per_device(states, stream):
-    tiles = pltpu.VMEM((FT, 8, 8, LANES), F32)
+    fine = pltpu.VMEM((FT, WIDE, LANES), F32)
+    coarse = pltpu.VMEM((CT, 2 * CROWS, LANES), F32)
 
     def tiled(x):
         return x.reshape(BAND // 8, 8, FT, LANES).transpose(0, 2, 1, 3)
@@ -433,11 +426,17 @@
         scratch_shapes=[
             pltpu.VMEM((WIDE // 8, FT, 8, LANES), F32),
             pltpu.VMEM((WIDE // 8, FT, 8, LANES), F32),
-            tiles, tiles, tiles, tiles, tiles, tiles, tiles,
+            fine,
+            pltpu.VMEM((STAGES + 1, FT, WIDE, LANES), F32),
+            fine,
+            fine,
             pltpu.VMEM((4 * LANES, LANES), jnp.bfloat16),
             pltpu.VMEM((LANES, 4 * LANES), jnp.bfloat16),
             pltpu.VMEM((2 * CT * 8, 4 * LANES), F32),
-            pltpu.VMEM((CT, 24, LANES), F32),
+            coarse,
+            coarse,
+            coarse,
+            pltpu.VMEM((5, CT, 2 * CROWS, LANES), F32),
             pltpu.VMEM((SLICES, CROWS, LANES), F32),
             pltpu.VMEM((SLICES, CROWS, LANES), F32),
             pltpu.VMEM((CWIDE, LANES), F32),

time: 36.8 us -> 64.1 us (1.74)
  Pallas kernels: 36 us -> 63.1 us
    pallas_call x1, Pallas kernels: 36 us -> 63.1 us  [per_device(): pl.pallas_call(kernel, out_shape=pltpu.VMEM((BAND // 8, FT, 8, LANES), F3...]
where the time goes in v4:
time: 64.1 us; the launch traced here: 63.9 us
  Pallas kernels  63.1 us (98%)
  local copies, waits for them, and re-layouts  0.71 us (1%)
    pallas_call x1, Pallas kernels, per_device(): pl.pallas_call(kernel, out_shape=pltpu.VMEM((BAND // 8, FT, 8, LANES), F3...  63.1 us

profile of v4, /device:TPU:1, one launch (start us, length us, event | category | flops | bytes accessed | tf_op | source)
XLA Modules:
  0.0 63.9 jit_solution(10400785208851201877)
XLA Ops:
  0.0 63.1 %shard_map.28 = f32[4,16,8,128]{3,2,1,0:T(8,128)S(1)} custom-call(f32[4,16,8,128]{3,2,1,0:T(8,128)} %bitcast.10, f32[4,16,8,128]{3,2,1,0:T(8,128)} %bitcast.11), custom_call_target="tpu_custom_call" | custom-call | tf_op jit(solution)/shard_map/pallas_call | solution.py:421
  63.1 0.7 %copy.4 = f32[1,32,2048]{2,1,0:T(8,128)} copy(f32[1,32,2048]{2,1,0:T(8,128)S(1)} %bitcast.9) | data formatting | bytes 524288

commit v5 on v4

--- a/solution.py
+++ b/solution.py
@@ -65,7 +65,7 @@
 
 def kernel(
     states, stream, out,
-    xwin, swin, psi, field, fce, fcn, shrink, grow, rows, cpsi, cce, ccn, cfield, wstream, wgap, spw, pay, nbuf, newc, spread_rows,
+    xwin, swin, psi, field, field1, field2, field3, fce, fcn, shrink, grow, rows, cpsi, cce, ccn, cfield, wstream, wgap, spw, pay, nbuf, newc, spread_rows,
     local_sem, halo_send, halo_recv, sc_send, sc_recv, a_send, a_recv, b_send, b_recv, c_send, c_recv,
 ):
     n = lax.axis_index("cuts")
@@ -211,8 +211,11 @@
         fce[c, pl.ds(*block)] = 0.25 - 0.3125 * (shifted(psi, c, block, 1) - shifted(psi, c, block, -1))
         fcn[c, pl.ds(*block)] = 0.25 + 0.3125 * (east - west)
 
-    def stage(at, base_at, s, blocks, tiles):
-        source, base, target = field.at[at], field.at[base_at], field.at[at + 1]
+    stages = [field, field1, field2, field3]
+
+    def stage(step, s, blocks, tiles):
+        source, base = stages[s].at[step], field.at[step]
+        target = stages[s + 1].at[step] if s < 3 else field.at[step + 1]
 
         def work(c, block, t, east, west):
             here = pl.ds(*block)
@@ -239,7 +242,7 @@
     by_runs(lambda tiles: over_tiles(psi, blocks_of(HALO + 1, HALO + BAND - 1), tiles, weigh))
     for k in range(STAGES - 1):
         inner = blocks_of(HALO + k + 1, HALO + BAND - k - 1)
-        by_runs(lambda tiles: stage(k, k // 4 * 4, k % 4, inner, tiles))
+        by_runs(lambda tiles: stage(k // 4, k % 4, inner, tiles))
 
     for halo in halos[:2]:
         halo.wait_recv()
@@ -278,11 +281,11 @@
         for s in range(4):
             done = 4 * step + s
             blocks = [(done + 1, HALO), (WIDE - HALO - 1 - done, HALO)]
-            stage(done, 4 * step, s, blocks, range(FT))
+            stage(step, s, blocks, range(FT))
         return carry
 
     lax.fori_loop(0, FINE_STEPS, fine_step, 0)
-    fine_end = field.at[STAGES]
+    fine_end = field.at[FINE_STEPS]
 
     ended = restricted_band(fine_end)
     gap = [ended[c] - coarse_old[c][...] for c in range(CT)]
@@ -413,6 +416,7 @@
 
 def per_device(states, stream):
     fine = pltpu.VMEM((FT, WIDE, LANES), F32)
+    by_step = pltpu.VMEM((FINE_STEPS, FT, WIDE, LANES), F32)
     coarse = pltpu.VMEM((CT, 2 * CROWS, LANES), F32)
 
     def tiled(x):
@@ -427,7 +431,8 @@
             pltpu.VMEM((WIDE // 8, FT, 8, LANES), F32),
             pltpu.VMEM((WIDE // 8, FT, 8, LANES), F32),
             fine,
-            pltpu.VMEM((STAGES + 1, FT, WIDE, LANES), F32),
+            pltpu.VMEM((FINE_STEPS + 1, FT, WIDE, LANES), F32),
+            by_step, by_step, by_step,
             fine,
             fine,
             pltpu.VMEM((4 * LANES, LANES), jnp.bfloat16),

time: 64.1 us -> 34.7 us (0.54)
  Pallas kernels: 63.1 us -> 33.9 us
    pallas_call x1, Pallas kernels: 63.1 us -> 33.9 us  [per_device(): pl.pallas_call(kernel, out_shape=pltpu.VMEM((BAND // 8, FT, 8, LANES), F3...]
where the time goes in v5:
time: 34.7 us; the launch traced here: 34.6 us
  Pallas kernels  33.9 us (98%)
  local copies, waits for them, and re-layouts  0.71 us (2%)
    pallas_call x1, Pallas kernels, per_device(): pl.pallas_call(kernel, out_shape=pltpu.VMEM((BAND // 8, FT, 8, LANES), F3...  33.9 us
    unnamed x1, local copies, waits for them, and re-layouts  0.71 us

profile of v5, /device:TPU:1, one launch (start us, length us, event | category | flops | bytes accessed | tf_op | source)
XLA Modules:
  0.0 34.6 jit_solution(6834152884048128562)
XLA Ops:
  0.0 33.9 %shard_map.28 = f32[4,16,8,128]{3,2,1,0:T(8,128)S(1)} custom-call(f32[4,16,8,128]{3,2,1,0:T(8,128)} %bitcast.10, f32[4,16,8,128]{3,2,1,0:T(8,128)} %bitcast.11), custom_call_target="tpu_custom_call" | custom-call | tf_op jit(solution)/shard_map/pallas_call | solution.py:425
  33.9 0.7 %copy.4 = f32[1,32,2048]{2,1,0:T(8,128)} copy(f32[1,32,2048]{2,1,0:T(8,128)S(1)} %bitcast.9) | data formatting | bytes 524288

commit v6 on v5

--- a/solution.py
+++ b/solution.py
@@ -85,8 +85,9 @@
         return (flipped(n, lax.rem(side + lax.rem(other // 2, 2), 2)), other)
 
     across = 2 * lax.rem(b, 2) - 1
-
-    offsets = [j for d in range(1, REACH + 1) for j in (-d, d)]
+    offsets = [(1, across)] + [(d, j) for d in range(2, REACH + 1) for j in (-d, d)] + [(1, -across)]
+    others = [lax.rem(n + k, SLICES) for k in (4, 5, 3, 2, 6, 1, 7)]
+
 
     own_x = pltpu.make_async_copy(states, xwin.at[pl.ds(HALO // 8, BAND // 8)], local_sem.at[0])
     own_s = pltpu.make_async_copy(stream, swin.at[pl.ds(HALO // 8, BAND // 8)], local_sem.at[1])
@@ -98,14 +99,14 @@
 
     barrier = pltpu.get_barrier_semaphore()
     greeted = [at_space(across)]
-    greeted += [(lax.rem(n + k, SLICES), b) for k in range(1, SLICES)]
-    greeted += [at_window(j) for j in reversed(offsets)]
+    greeted += [(k, b) for k in others]
+    greeted += [at_window(j) for _, j in offsets]
     for device in greeted:
         pl.semaphore_signal(barrier, inc=1, device_id=device, device_id_type=MESH)
     pl.semaphore_wait(barrier, len(greeted))
 
     halos = []
-    for at, (source, window, device) in enumerate(((stream, swin, at_window), (states, xwin, at_space))):
+    for at, (source, window, device) in enumerate(((stream, swin, at_space), (states, xwin, at_space))):
         for end, (j, first, target) in enumerate(((1, BAND - HALO, 0), (-1, 0, HALO + BAND))):
             halos.append(
                 pltpu.make_async_remote_copy(
@@ -163,11 +164,11 @@
     untile(swin, psi, own)
     windows(restricted_band(psi), wstream)
     spreads = []
-    for at, j in enumerate(offsets):
+    for at, (_, j) in enumerate(offsets):
         spreads.append(
             pltpu.make_async_remote_copy(
                 src_ref=wstream.at[column],
-                dst_ref=spw.at[pl.ds(CROWS * (REACH - j), CROWS)],
+                dst_ref=spw.at[pl.ds(pl.multiple_of(CROWS * (REACH - j), CROWS), CROWS)],
                 send_sem=sc_send.at[at],
                 recv_sem=sc_recv.at[at],
                 device_id=at_window(j),
@@ -281,7 +282,7 @@
         for s in range(4):
             done = 4 * step + s
             blocks = [(done + 1, HALO), (WIDE - HALO - 1 - done, HALO)]
-            stage(step, s, blocks, range(FT))
+            stage(step, s, blocks, [(c + s) % FT for c in range(FT)])
         return carry
 
     lax.fori_loop(0, FINE_STEPS, fine_step, 0)
@@ -303,13 +304,10 @@
             device_id_type=MESH,
         )
 
-    for k in range(SLICES):
-        @pl.when((n != k) & (n < SLICES - 1))
-        def _():
-            gap_copy(k, n).start()
-
     @pl.when(n < SLICES - 1)
     def _():
+        for k in others:
+            gap_copy(k, n).start()
         pay[n, middle] = wgap[column]
 
     for spread in spreads:
@@ -326,12 +324,12 @@
             gap_copy(m, m).wait_recv()
 
     gathers = []
-    for at, j in enumerate(offsets):
-        count = SLICES + 1 - 2 * abs(j)
+    for at, (distance, j) in enumerate(offsets):
+        count = SLICES + 1 - 2 * distance
         gathers.append(
             pltpu.make_async_remote_copy(
                 src_ref=pay.at[pl.ds(0, count), middle],
-                dst_ref=pay.at[pl.ds(0, count), pl.ds(CROWS * (REACH - j), CROWS)],
+                dst_ref=pay.at[pl.ds(0, count), pl.ds(pl.multiple_of(CROWS * (REACH - j), CROWS), CROWS)],
                 send_sem=b_send.at[at],
                 recv_sem=b_recv.at[at],
                 device_id=at_window(j),
@@ -339,6 +337,14 @@
             )
         )
         gathers[-1].start()
+
+    for halo in halos:
+        halo.wait_send()
+
+    @pl.when(n < SLICES - 1)
+    def _():
+        for k in others:
+            gap_copy(k, n).wait_send()
 
     for gather in gathers:
         gather.wait_recv()
@@ -376,6 +382,13 @@
 
     first = jnp.stack([pay[0, pl.ds(4 + r, 8, stride=8)] for r in range(8)])
     lax.fori_loop(1, SLICES, link, first)
+
+    for gather in gathers:
+        gather.wait_send()
+    for i in range(1, SLICES):
+        @pl.when(n != i)
+        def _():
+            new_copy(i, column).wait_send()
 
     for k in range(SLICES):
         @pl.when((n != k) & (n > 0))
@@ -399,19 +412,6 @@
                     fine_end[4 * c + m, pl.ds(HALO + 8 * i, 8)]
                     + fine_change[BAND * c + 8 * i:BAND * c + 8 * (i + 1), m * LANES:(m + 1) * LANES]
                 )
-
-    for halo in halos:
-        halo.wait_send()
-    for k in range(SLICES):
-        @pl.when((n != k) & (n < SLICES - 1))
-        def _():
-            gap_copy(k, n).wait_send()
-    for gather in gathers:
-        gather.wait_send()
-    for i in range(1, SLICES):
-        @pl.when(n != i)
-        def _():
-            new_copy(i, column).wait_send()
 
 
 def per_device(states, stream):

time: 34.7 us -> 34.7 us (level)
  no operation moved by 1% of the time
where the time goes in v6:
time: 34.7 us; the launch traced here: 34.6 us
  Pallas kernels  33.9 us (98%)
  local copies, waits for them, and re-layouts  0.71 us (2%)
    pallas_call x1, Pallas kernels, per_device(): pl.pallas_call(kernel, out_shape=pltpu.VMEM((BAND // 8, FT, 8, LANES), F3...  33.9 us
    unnamed x1, local copies, waits for them, and re-layouts  0.71 us

profile of v6, /device:TPU:1, one launch (start us, length us, event | category | flops | bytes accessed | tf_op | source)
XLA Modules:
  0.0 34.6 jit_solution(11845316115131445884)
XLA Ops:
  0.0 33.9 %shard_map.28 = f32[4,16,8,128]{3,2,1,0:T(8,128)S(1)} custom-call(f32[4,16,8,128]{3,2,1,0:T(8,128)} %bitcast.10, f32[4,16,8,128]{3,2,1,0:T(8,128)} %bitcast.11), custom_call_target="tpu_custom_call" | custom-call | tf_op jit(solution)/shard_map/pallas_call | solution.py:425
  33.9 0.7 %copy.4 = f32[1,32,2048]{2,1,0:T(8,128)} copy(f32[1,32,2048]{2,1,0:T(8,128)S(1)} %bitcast.9) | data formatting | bytes 524288

commit v7 on v6

--- a/solution.py
+++ b/solution.py
@@ -278,14 +278,11 @@
                 cfield[s + 1, c, here] = COARSE_BETAS[s] * cfield[0, c, here] + change
     coarse_old = [cfield.at[4, c, pl.ds(4, CROWS)] for c in range(CT)]
 
-    def fine_step(step, carry):
+    for step in range(FINE_STEPS):
         for s in range(4):
             done = 4 * step + s
             blocks = [(done + 1, HALO), (WIDE - HALO - 1 - done, HALO)]
             stage(step, s, blocks, [(c + s) % FT for c in range(FT)])
-        return carry
-
-    lax.fori_loop(0, FINE_STEPS, fine_step, 0)
     fine_end = field.at[FINE_STEPS]
 
     ended = restricted_band(fine_end)

time: 34.7 us -> 33.3 us (0.960)
  Pallas kernels: 33.9 us -> 32.5 us
    pallas_call x1, Pallas kernels: 33.9 us -> 32.5 us  [per_device(): pl.pallas_call(kernel, out_shape=pltpu.VMEM((BAND // 8, FT, 8, LANES), F3...]
where the time goes in v7:
time: 33.3 us; the launch traced here: 33.2 us
  Pallas kernels  32.5 us (98%)
  local copies, waits for them, and re-layouts  0.71 us (2%)
    pallas_call x1, Pallas kernels, per_device(): pl.pallas_call(kernel, out_shape=pltpu.VMEM((BAND // 8, FT, 8, LANES), F3...  32.5 us
    unnamed x1, local copies, waits for them, and re-layouts  0.71 us

profile of v7, /device:TPU:1, one launch (start us, length us, event | category | flops | bytes accessed | tf_op | source)
XLA Modules:
  0.0 33.2 jit_solution(5414730699955076098)
XLA Ops:
  0.0 32.5 %shard_map.28 = f32[4,16,8,128]{3,2,1,0:T(8,128)S(1)} custom-call(f32[4,16,8,128]{3,2,1,0:T(8,128)} %bitcast.10, f32[4,16,8,128]{3,2,1,0:T(8,128)} %bitcast.11), custom_call_target="tpu_custom_call" | custom-call | tf_op jit(solution)/shard_map/pallas_call | solution.py:422
  32.5 0.7 %copy.4 = f32[1,32,2048]{2,1,0:T(8,128)} copy(f32[1,32,2048]{2,1,0:T(8,128)S(1)} %bitcast.9) | data formatting | bytes 524288

commit v8 on v7

--- a/solution.py
+++ b/solution.py
@@ -221,7 +221,7 @@
         def work(c, block, t, east, west):
             here = pl.ds(*block)
             up, down = shifted(source, c, block, 1), shifted(source, c, block, -1)
-            change = fcn[c, here] * (up - down) + (0.5 * (west + down) - t) + fce[c, here] * (east - west)
+            change = (fcn[c, here] * (up - down) + (0.5 * down - t)) + (fce[c, here] * (east - west) + 0.5 * west)
             if s == 0:
                 change = FINE_START * change
             target[c, here] = FINE_BETAS[s] * base[c, here] + change

time: 33.3 us -> 33.2 us (level)
  no operation moved by 1% of the time
where the time goes in v8:
time: 33.2 us; the launch traced here: 33.1 us
  Pallas kernels  32.4 us (98%)
  local copies, waits for them, and re-layouts  0.71 us (2%)
    pallas_call x1, Pallas kernels, per_device(): pl.pallas_call(kernel, out_shape=pltpu.VMEM((BAND // 8, FT, 8, LANES), F3...  32.4 us
    unnamed x1, local copies, waits for them, and re-layouts  0.71 us

profile of v8, /device:TPU:1, one launch (start us, length us, event | category | flops | bytes accessed | tf_op | source)
XLA Modules:
  0.0 33.1 jit_solution(12081306443774220124)
XLA Ops:
  0.0 32.4 %shard_map.28 = f32[4,16,8,128]{3,2,1,0:T(8,128)S(1)} custom-call(f32[4,16,8,128]{3,2,1,0:T(8,128)} %bitcast.10, f32[4,16,8,128]{3,2,1,0:T(8,128)} %bitcast.11), custom_call_target="tpu_custom_call" | custom-call | tf_op jit(solution)/shard_map/pallas_call | solution.py:422
  32.4 0.7 %copy.4 = f32[1,32,2048]{2,1,0:T(8,128)} copy(f32[1,32,2048]{2,1,0:T(8,128)S(1)} %bitcast.9) | data formatting | bytes 524288

commit v9 on v8

--- a/solution.py
+++ b/solution.py
@@ -272,7 +272,7 @@
                 west = jnp.where(first_lane(t[1]), pltpu.roll(t[0], 1, 1), pltpu.roll(t[1], 1, 1))
                 east = jnp.where(last_lane(t[1]), pltpu.roll(t[2], LANES - 1, 1), pltpu.roll(t[1], LANES - 1, 1))
                 up, down = shifted(cfield.at[s], c, block, 1), shifted(cfield.at[s], c, block, -1)
-                change = ccn[c, here] * (up - down) + (0.5 * (west + down) - t[1]) + cce[c, here] * (east - west)
+                change = (ccn[c, here] * (up - down) + (0.5 * down - t[1])) + (cce[c, here] * (east - west) + 0.5 * west)
                 if s == 0:
                     change = COARSE_START * change
                 cfield[s + 1, c, here] = COARSE_BETAS[s] * cfield[0, c, here] + change
@@ -359,10 +359,13 @@
     def link(i, current):
         t = current
         for s in range(4):
-            change = operator(t, pltpu.roll(t, LANES - 1, 2), pltpu.roll(t, 1, 2), *chain_weights)
+            ce, cw, cn, cs = chain_weights
+            east, west = pltpu.roll(t, LANES - 1, 2), pltpu.roll(t, 1, 2)
+            rest, turned = cn * rows_up(t) + cs * rows_down(t) - t, ce * east + cw * west
             if s == 0:
-                change = COARSE_START * change
-            t = COARSE_BETAS[s] * current + change
+                t = COARSE_BETAS[s] * current + COARSE_START * (rest + turned)
+            else:
+                t = (COARSE_BETAS[s] * current + rest) + turned
         for r in range(8):
             nbuf[i, pl.ds(4 + r, 8, stride=8)] = t[r]
 

time: 33.2 us -> 33.2 us (level)
  no operation moved by 1% of the time
where the time goes in v9:
time: 33.2 us; the launch traced here: 33.1 us
  Pallas kernels  32.3 us (97%)
  local copies, waits for them, and re-layouts  0.71 us (2%)
    pallas_call x1, Pallas kernels, per_device(): pl.pallas_call(kernel, out_shape=pltpu.VMEM((BAND // 8, FT, 8, LANES), F3...  32.3 us
    unnamed x1, local copies, waits for them, and re-layouts  0.71 us

profile of v9, /device:TPU:1, one launch (start us, length us, event | category | flops | bytes accessed | tf_op | source)
XLA Modules:
  0.0 33.1 jit_solution(16768412307109554734)
XLA Ops:
  0.0 32.3 %shard_map.28 = f32[4,16,8,128]{3,2,1,0:T(8,128)S(1)} custom-call(f32[4,16,8,128]{3,2,1,0:T(8,128)} %bitcast.10, f32[4,16,8,128]{3,2,1,0:T(8,128)} %bitcast.11), custom_call_target="tpu_custom_call" | custom-call | tf_op jit(solution)/shard_map/pallas_call | solution.py:425
  32.3 0.7 %copy.4 = f32[1,32,2048]{2,1,0:T(8,128)} copy(f32[1,32,2048]{2,1,0:T(8,128)S(1)} %bitcast.9) | data formatting | bytes 524288
